TPU v7x, 512 devices: a whole 4x4x16 slice. The times are simulated.
512 devices in a mesh: section: 16 (over x, z_hi, core), dp: 32 (over y, z_lo).
Axes of the slice: x: 4, y: 4, z: 16 (z_hi: 2, z_lo: 8; z = z_hi * 8 + z_lo), core: 2. Of those that a mesh axis runs over, the one named last changes fastest.
Arguments:
- section_inputs: bfloat16 [16, 2, 2048, 4096], P('section', None, 'dp'), may hold values from -6 to 6
- loss_grads: bfloat16 [2, 2048, 4096], P(None, 'dp'), may hold values from -384 to 384
- weight_codes: int32 [2, 2048], P(None, 'dp'), may hold values from 0 to 127, as said below
- proj_weight: bfloat16 [16, 4096, 512], P('section', 'dp'), may hold values from -0.09375 to 0.09375
Outputs:
- weight_grads: float32 [16, 4096, 512], P('section', 'dp')
Inputs may be any that keep to these rules, and one draw needn't show every extreme that they name: `weight_codes`: the weight of a token is its code / 127.
All inputs are finite; a program needn't handle non-finite values.
Results may differ from a plain program's by a relative error of at most 0.035.
Values may be sent and summed in bfloat16 or wider, within the bound.
A program may use at most 128 MiB of HBM per device.

v0:
```python
import jax
import jax.numpy as jnp
from jax import lax
from jax.sharding import PartitionSpec as P

epsilon = 1e-06


def shifted(block, axis, distance):
    devices = range(lax.axis_size(axis))
    route = [(i - distance, i) for i in devices if i - distance in devices]
    return lax.ppermute(block, axis, route)


def section_backward(inputs, grad_output, weight):
    values = inputs.astype(jnp.float32)
    inv_rms = lax.rsqrt(jnp.mean(values * values, axis=-1, keepdims=True) + epsilon)
    unit_rows = values * inv_rms
    normed = unit_rows.astype(jnp.bfloat16)
    project = jnp.dot(normed, weight, preferred_element_type=jnp.float32)
    activated = jax.nn.silu(project).astype(jnp.bfloat16)
    grad_act = jnp.dot(grad_output, weight, preferred_element_type=jnp.float32)
    gate_prob = jax.nn.sigmoid(project)
    grad_proj = (grad_act * gate_prob * (1.0 + project * (1.0 - gate_prob))).astype(jnp.bfloat16)
    grad_norm = lax.dot_general(
        grad_proj, weight, (((1,), (1,)), ((), ())), preferred_element_type=jnp.float32
    )
    grad_rows = inv_rms * (
        grad_norm - unit_rows * jnp.mean(grad_norm * unit_rows, axis=-1, keepdims=True)
    )
    grad_input = (grad_output.astype(jnp.float32) + grad_rows).astype(jnp.bfloat16)
    return (grad_input, normed, grad_proj, activated)


def weight_term(normed, grad_proj, grad_output, activated):
    dims = (((0,), (0,)), ((), ()))
    first = lax.dot_general(normed, grad_proj, dims, preferred_element_type=jnp.float32)
    return first + lax.dot_general(grad_output, activated, dims, preferred_element_type=jnp.float32)


def shards(section_inputs, loss_grads, weight_codes, proj_weight):
    sections = lax.axis_size("section")
    place = lax.axis_index("section")
    inputs = section_inputs[0]
    batches, tok_rows, width = inputs.shape
    code_values = weight_codes.astype(jnp.float32)
    weight_total = lax.psum(jnp.sum(code_values), "dp") / 127.0
    seed_grads = (
        loss_grads.astype(jnp.float32) * (code_values / 127.0)[:, :, None] / weight_total
    ).astype(jnp.bfloat16)
    weight = lax.all_gather(proj_weight[0], "dp", axis=0, tiled=True)
    hidden = weight.shape[1]
    summed = jnp.zeros((8, 128), jnp.float32)
    wide_record = jnp.zeros((batches, tok_rows, width), jnp.bfloat16)
    narrow_record = jnp.zeros((batches, tok_rows, hidden), jnp.bfloat16)
    state = (wide_record, wide_record, narrow_record, narrow_record, summed)

    def advance(step_index, incoming, state):
        batch = step_index - (sections - 1 - place)
        active = jnp.logical_and(batch >= 0, batch < batches)
        slot = jnp.clip(batch, 0, batches - 1)
        seeded = lax.dynamic_index_in_dim(seed_grads, slot, 0, keepdims=False)
        grad_output = jnp.where(place == sections - 1, seeded, incoming)
        rows = lax.dynamic_index_in_dim(inputs, slot, 0, keepdims=False)

        def work(state):
            grad_input, normed, grad_proj, activated = section_backward(rows, grad_output, weight)
            outs_record, norm_record, proj_record, act_record, total = state
            outs_record = lax.dynamic_update_index_in_dim(outs_record, grad_output, slot, 0)
            norm_record = lax.dynamic_update_index_in_dim(norm_record, normed, slot, 0)
            proj_record = lax.dynamic_update_index_in_dim(proj_record, grad_proj, slot, 0)
            act_record = lax.dynamic_update_index_in_dim(act_record, activated, slot, 0)
            return (grad_input, (outs_record, norm_record, proj_record, act_record, total))

        def resting(state):
            return (jnp.zeros_like(incoming), state)

        return lax.cond(active, work, resting, state)

    def loop_step(step_index, carry):
        incoming, state = carry
        outgoing, state = advance(step_index, incoming, state)
        incoming = shifted(outgoing, "section", -1)
        return (incoming, state)

    final_step = batches + sections - 2
    starting = jnp.zeros((tok_rows, width), jnp.bfloat16)
    incoming, state = lax.fori_loop(0, final_step, loop_step, (starting, state))
    outgoing, state = advance(final_step, incoming, state)
    outs_record, norm_record, proj_record, act_record, summed = state
    flat_outs = outs_record.reshape(batches * tok_rows, width)
    flat_norm = norm_record.reshape(batches * tok_rows, width)
    flat_proj = proj_record.reshape(batches * tok_rows, hidden)
    flat_act = act_record.reshape(batches * tok_rows, hidden)
    partial_sum = weight_term(flat_norm, flat_proj, flat_outs, flat_act)
    grads = lax.psum_scatter(
        partial_sum.astype(jnp.bfloat16), "dp", scatter_dimension=0, tiled=True
    ).astype(jnp.float32)
    return grads[None]


def solution(mesh):
    return jax.shard_map(
        shards,
        mesh=mesh,
        in_specs=(
            P("section", None, "dp", None),
            P(None, "dp", None),
            P(None, "dp"),
            P("section", "dp", None),
        ),
        out_specs=P("section", "dp", None),
        check_vma=False,
    )
```

profile of v0, /device:TPU:6, one launch (start us, length us, event | category | flops | bytes accessed | tf_op | source)
XLA Modules:
  0.0 1031.6 jit_solution(9468676819730700049)
XLA Ops:
  6.5 0.7 all-gather.3.cloned.1.call-update
  7.3 1.3 convert_multiply_fusion.1
  8.6 129.0 %psum.7 = f32[]{:T(128)} all-reduce(f32[]{:T(128)} %get-tuple-element.537), channel_id=1, replica_groups=mesh['section'=16,'dp'=32] {'dp'}, use_global_device_ids=true, to_apply=%region_1.0 | all-reduce | flops 1 | bytes 8 | tf_op jit(solution)/shard_map/psum | solution.py:47
  138.2 1.6 divide_convert_fusion
  139.7 118.8 %all-gather.3.cloned.1.call-done = bf16[1,4096,512]{2,1,0:T(8,128)(2,1)} async-done(((bf16[1,128,512]{2,1,0:T(8,128)(2,1)}), bf16[1,4096,512]{2,1,0:T(8,128)(2,1)}) %all-gather.3.cloned.1.call-update) | async-done | bytes 4194320 | tf_op jit(solution)/shard_map/all_gather | solution.py:51
  258.5 1.1 broadcast_in_dim.52.clone
  259.6 1.1 broadcast_in_dim.52
  260.7 405.8 %while.23 = (s32[]{:T(128)}, bf16[64,4096]{1,0:T(8,128)(2,1)S(1)}, bf16[2,64,4096]{2,1,0:T(8,128)(2,1)}, bf16[2,64,4096]{2,1,0:T(8,128)(2,1)}, bf16[2,64,512]{2,...) while((s32[]{:T(128)}, bf16[64,4096]{1,0:T(8,128)(2,1)S(1)}, ...), condition=%wide.region_7.8_spmd, body=%wide.region_2.7_spmd.sunk | while | flops 811532352 | bytes 57676576 | solution.py:88
  260.7 0.1 conditional.4
  260.8 1.9 collective-permute-start
  262.7 10.3 %collective-permute-done = bf16[64,4096]{1,0:T(8,128)(2,1)S(1)} collective-permute-done((bf16[64,4096]{1,0:T(8,128)(2,1)S(1)}, bf16[64,4096]{1,0:T(8,128)(2,1)S(1)}, u32[]{:S(2)}, u32[]{:S(2)}) %collective-permute-start) | collective-permute-done | bytes 524320 | tf_op jit(solution)/shard_map/while/body/eval_jaxpr/ppermute | solution.py:12
  273.0 0.1 conditional.4
  273.1 13.6 %collective-permute-start = (bf16[64,4096]{1,0:T(8,128)(2,1)S(1)}, bf16[64,4096]{1,0:T(8,128)(2,1)S(1)}, u32[]{:S(2)}, u32[]{:S(2)}) collective-permute-start(bf16[64,4096]{1,0:T(8,128)(2,1)S(1)} %get-tuple-element.610), channel_id=1, source_target_pairs={{32,0},{64,32},{96,64},{128,96},{160,128},{192,160},{224,192},{256... | collective-permute-start | bytes 1572872 | tf_op jit(solution)/shard_map/while/body/eval_jaxpr/ppermute | solution.py:12
  286.7 9.2 collective-permute-done
  295.9 0.1 conditional.4
  295.9 13.6 %collective-permute-start = (bf16[64,4096]{1,0:T(8,128)(2,1)S(1)}, bf16[64,4096]{1,0:T(8,128)(2,1)S(1)}, u32[]{:S(2)}, u32[]{:S(2)}) collective-permute-start(bf16[64,4096]{1,0:T(8,128)(2,1)S(1)} %get-tuple-element.610), channel_id=1, source_target_pairs={{32,0},{64,32},{96,64},{128,96},{160,128},{192,160},{224,192},{256... | collective-permute-start | bytes 1572872 | tf_op jit(solution)/shard_map/while/body/eval_jaxpr/ppermute | solution.py:12
  309.6 12.7 %collective-permute-done = bf16[64,4096]{1,0:T(8,128)(2,1)S(1)} collective-permute-done((bf16[64,4096]{1,0:T(8,128)(2,1)S(1)}, bf16[64,4096]{1,0:T(8,128)(2,1)S(1)}, u32[]{:S(2)}, u32[]{:S(2)}) %collective-permute-start) | collective-permute-done | bytes 524320 | tf_op jit(solution)/shard_map/while/body/eval_jaxpr/ppermute | solution.py:12
  322.3 6.8 conditional.4
  322.3 0.2 fusion.12
  322.5 3.3 bitcast_dynamic-update-slice_fusion.1
  325.8 0.3 bitcast_dynamic-update-slice_fusion
  326.1 0.3 copy-done
  326.4 0.8 bitcast_dynamic-update-slice_fusion.2
  327.2 1.5 fusion.7
  328.7 0.3 fusion.11
  329.1 6.9 collective-permute-start
  336.0 12.5 %collective-permute-done = bf16[64,4096]{1,0:T(8,128)(2,1)S(1)} collective-permute-done((bf16[64,4096]{1,0:T(8,128)(2,1)S(1)}, bf16[64,4096]{1,0:T(8,128)(2,1)S(1)}, u32[]{:S(2)}, u32[]{:S(2)}) %collective-permute-start) | collective-permute-done | bytes 524320 | tf_op jit(solution)/shard_map/while/body/eval_jaxpr/ppermute | solution.py:12
  348.5 6.8 conditional.4
  348.5 0.2 fusion.12
  348.7 3.3 bitcast_dynamic-update-slice_fusion.1
  352.0 0.3 bitcast_dynamic-update-slice_fusion
  352.3 0.3 copy-done
  352.6 0.8 bitcast_dynamic-update-slice_fusion.2
  353.4 1.5 fusion.7
  354.9 0.3 fusion.11
  355.3 13.5 %collective-permute-start = (bf16[64,4096]{1,0:T(8,128)(2,1)S(1)}, bf16[64,4096]{1,0:T(8,128)(2,1)S(1)}, u32[]{:S(2)}, u32[]{:S(2)}) collective-permute-start(bf16[64,4096]{1,0:T(8,128)(2,1)S(1)} %get-tuple-element.610), channel_id=1, source_target_pairs={{32,0},{64,32},{96,64},{128,96},{160,128},{192,160},{224,192},{256... | collective-permute-start | bytes 1572872 | tf_op jit(solution)/shard_map/while/body/eval_jaxpr/ppermute | solution.py:12
  368.8 8.2 collective-permute-done
  377.0 0.1 conditional.4
  377.1 20.2 %collective-permute-start = (bf16[64,4096]{1,0:T(8,128)(2,1)S(1)}, bf16[64,4096]{1,0:T(8,128)(2,1)S(1)}, u32[]{:S(2)}, u32[]{:S(2)}) collective-permute-start(bf16[64,4096]{1,0:T(8,128)(2,1)S(1)} %get-tuple-element.610), channel_id=1, source_target_pairs={{32,0},{64,32},{96,64},{128,96},{160,128},{192,160},{224,192},{256... | collective-permute-start | bytes 1572872 | tf_op jit(solution)/shard_map/while/body/eval_jaxpr/ppermute | solution.py:12
  397.3 6.9 collective-permute-done
  404.2 13.5 %collective-permute-start = (bf16[64,4096]{1,0:T(8,128)(2,1)S(1)}, bf16[64,4096]{1,0:T(8,128)(2,1)S(1)}, u32[]{:S(2)}, u32[]{:S(2)}) collective-permute-start(bf16[64,4096]{1,0:T(8,128)(2,1)S(1)} %get-tuple-element.610), channel_id=1, source_target_pairs={{32,0},{64,32},{96,64},{128,96},{160,128},{192,160},{224,192},{256... | collective-permute-start | bytes 1572872 | tf_op jit(solution)/shard_map/while/body/eval_jaxpr/ppermute | solution.py:12
  417.8 13.5 %collective-permute-done = bf16[64,4096]{1,0:T(8,128)(2,1)S(1)} collective-permute-done((bf16[64,4096]{1,0:T(8,128)(2,1)S(1)}, bf16[64,4096]{1,0:T(8,128)(2,1)S(1)}, u32[]{:S(2)}, u32[]{:S(2)}) %collective-permute-start) | collective-permute-done | bytes 524320 | tf_op jit(solution)/shard_map/while/body/eval_jaxpr/ppermute | solution.py:12
  431.3 13.5 %collective-permute-start = (bf16[64,4096]{1,0:T(8,128)(2,1)S(1)}, bf16[64,4096]{1,0:T(8,128)(2,1)S(1)}, u32[]{:S(2)}, u32[]{:S(2)}) collective-permute-start(bf16[64,4096]{1,0:T(8,128)(2,1)S(1)} %get-tuple-element.610), channel_id=1, source_target_pairs={{32,0},{64,32},{96,64},{128,96},{160,128},{192,160},{224,192},{256... | collective-permute-start | bytes 1572872 | tf_op jit(solution)/shard_map/while/body/eval_jaxpr/ppermute | solution.py:12
  444.8 13.8 %collective-permute-done = bf16[64,4096]{1,0:T(8,128)(2,1)S(1)} collective-permute-done((bf16[64,4096]{1,0:T(8,128)(2,1)S(1)}, bf16[64,4096]{1,0:T(8,128)(2,1)S(1)}, u32[]{:S(2)}, u32[]{:S(2)}) %collective-permute-start) | collective-permute-done | bytes 524320 | tf_op jit(solution)/shard_map/while/body/eval_jaxpr/ppermute | solution.py:12
  458.7 13.6 %collective-permute-start = (bf16[64,4096]{1,0:T(8,128)(2,1)S(1)}, bf16[64,4096]{1,0:T(8,128)(2,1)S(1)}, u32[]{:S(2)}, u32[]{:S(2)}) collective-permute-start(bf16[64,4096]{1,0:T(8,128)(2,1)S(1)} %get-tuple-element.610), channel_id=1, source_target_pairs={{32,0},{64,32},{96,64},{128,96},{160,128},{192,160},{224,192},{256... | collective-permute-start | bytes 1572872 | tf_op jit(solution)/shard_map/while/body/eval_jaxpr/ppermute | solution.py:12
  472.3 13.6 %collective-permute-done = bf16[64,4096]{1,0:T(8,128)(2,1)S(1)} collective-permute-done((bf16[64,4096]{1,0:T(8,128)(2,1)S(1)}, bf16[64,4096]{1,0:T(8,128)(2,1)S(1)}, u32[]{:S(2)}, u32[]{:S(2)}) %collective-permute-start) | collective-permute-done | bytes 524320 | tf_op jit(solution)/shard_map/while/body/eval_jaxpr/ppermute | solution.py:12
  486.0 13.5 %collective-permute-start = (bf16[64,4096]{1,0:T(8,128)(2,1)S(1)}, bf16[64,4096]{1,0:T(8,128)(2,1)S(1)}, u32[]{:S(2)}, u32[]{:S(2)}) collective-permute-start(bf16[64,4096]{1,0:T(8,128)(2,1)S(1)} %get-tuple-element.610), channel_id=1, source_target_pairs={{32,0},{64,32},{96,64},{128,96},{160,128},{192,160},{224,192},{256... | collective-permute-start | bytes 1572872 | tf_op jit(solution)/shard_map/while/body/eval_jaxpr/ppermute | solution.py:12
  499.5 13.7 %collective-permute-done = bf16[64,4096]{1,0:T(8,128)(2,1)S(1)} collective-permute-done((bf16[64,4096]{1,0:T(8,128)(2,1)S(1)}, bf16[64,4096]{1,0:T(8,128)(2,1)S(1)}, u32[]{:S(2)}, u32[]{:S(2)}) %collective-permute-start) | collective-permute-done | bytes 524320 | tf_op jit(solution)/shard_map/while/body/eval_jaxpr/ppermute | solution.py:12
  513.3 13.4 %collective-permute-start = (bf16[64,4096]{1,0:T(8,128)(2,1)S(1)}, bf16[64,4096]{1,0:T(8,128)(2,1)S(1)}, u32[]{:S(2)}, u32[]{:S(2)}) collective-permute-start(bf16[64,4096]{1,0:T(8,128)(2,1)S(1)} %get-tuple-element.610), channel_id=1, source_target_pairs={{32,0},{64,32},{96,64},{128,96},{160,128},{192,160},{224,192},{256... | collective-permute-start | bytes 1572872 | tf_op jit(solution)/shard_map/while/body/eval_jaxpr/ppermute | solution.py:12
  526.7 13.0 %collective-permute-done = bf16[64,4096]{1,0:T(8,128)(2,1)S(1)} collective-permute-done((bf16[64,4096]{1,0:T(8,128)(2,1)S(1)}, bf16[64,4096]{1,0:T(8,128)(2,1)S(1)}, u32[]{:S(2)}, u32[]{:S(2)}) %collective-permute-start) | collective-permute-done | bytes 524320 | tf_op jit(solution)/shard_map/while/body/eval_jaxpr/ppermute | solution.py:12
  539.8 13.7 %collective-permute-start = (bf16[64,4096]{1,0:T(8,128)(2,1)S(1)}, bf16[64,4096]{1,0:T(8,128)(2,1)S(1)}, u32[]{:S(2)}, u32[]{:S(2)}) collective-permute-start(bf16[64,4096]{1,0:T(8,128)(2,1)S(1)} %get-tuple-element.610), channel_id=1, source_target_pairs={{32,0},{64,32},{96,64},{128,96},{160,128},{192,160},{224,192},{256... | collective-permute-start | bytes 1572872 | tf_op jit(solution)/shard_map/while/body/eval_jaxpr/ppermute | solution.py:12
  553.4 6.7 collective-permute-done
  560.2 13.6 %collective-permute-start = (bf16[64,4096]{1,0:T(8,128)(2,1)S(1)}, bf16[64,4096]{1,0:T(8,128)(2,1)S(1)}, u32[]{:S(2)}, u32[]{:S(2)}) collective-permute-start(bf16[64,4096]{1,0:T(8,128)(2,1)S(1)} %get-tuple-element.610), channel_id=1, source_target_pairs={{32,0},{64,32},{96,64},{128,96},{160,128},{192,160},{224,192},{256... | collective-permute-start | bytes 1572872 | tf_op jit(solution)/shard_map/while/body/eval_jaxpr/ppermute | solution.py:12
  573.7 12.2 %collective-permute-done = bf16[64,4096]{1,0:T(8,128)(2,1)S(1)} collective-permute-done((bf16[64,4096]{1,0:T(8,128)(2,1)S(1)}, bf16[64,4096]{1,0:T(8,128)(2,1)S(1)}, u32[]{:S(2)}, u32[]{:S(2)}) %collective-permute-start) | collective-permute-done | bytes 524320 | tf_op jit(solution)/shard_map/while/body/eval_jaxpr/ppermute | solution.py:12
  586.0 13.6 %collective-permute-start = (bf16[64,4096]{1,0:T(8,128)(2,1)S(1)}, bf16[64,4096]{1,0:T(8,128)(2,1)S(1)}, u32[]{:S(2)}, u32[]{:S(2)}) collective-permute-start(bf16[64,4096]{1,0:T(8,128)(2,1)S(1)} %get-tuple-element.610), channel_id=1, source_target_pairs={{32,0},{64,32},{96,64},{128,96},{160,128},{192,160},{224,192},{256... | collective-permute-start | bytes 1572872 | tf_op jit(solution)/shard_map/while/body/eval_jaxpr/ppermute | solution.py:12
  599.6 12.4 %collective-permute-done = bf16[64,4096]{1,0:T(8,128)(2,1)S(1)} collective-permute-done((bf16[64,4096]{1,0:T(8,128)(2,1)S(1)}, bf16[64,4096]{1,0:T(8,128)(2,1)S(1)}, u32[]{:S(2)}, u32[]{:S(2)}) %collective-permute-start) | collective-permute-done | bytes 524320 | tf_op jit(solution)/shard_map/while/body/eval_jaxpr/ppermute | solution.py:12
  612.1 13.5 %collective-permute-start = (bf16[64,4096]{1,0:T(8,128)(2,1)S(1)}, bf16[64,4096]{1,0:T(8,128)(2,1)S(1)}, u32[]{:S(2)}, u32[]{:S(2)}) collective-permute-start(bf16[64,4096]{1,0:T(8,128)(2,1)S(1)} %get-tuple-element.610), channel_id=1, source_target_pairs={{32,0},{64,32},{96,64},{128,96},{160,128},{192,160},{224,192},{256... | collective-permute-start | bytes 1572872 | tf_op jit(solution)/shard_map/while/body/eval_jaxpr/ppermute | solution.py:12
  625.6 14.9 %collective-permute-done = bf16[64,4096]{1,0:T(8,128)(2,1)S(1)} collective-permute-done((bf16[64,4096]{1,0:T(8,128)(2,1)S(1)}, bf16[64,4096]{1,0:T(8,128)(2,1)S(1)}, u32[]{:S(2)}, u32[]{:S(2)}) %collective-permute-start) | collective-permute-done | bytes 524320 | tf_op jit(solution)/shard_map/while/body/eval_jaxpr/ppermute | solution.py:12
  640.5 13.6 %collective-permute-start = (bf16[64,4096]{1,0:T(8,128)(2,1)S(1)}, bf16[64,4096]{1,0:T(8,128)(2,1)S(1)}, u32[]{:S(2)}, u32[]{:S(2)}) collective-permute-start(bf16[64,4096]{1,0:T(8,128)(2,1)S(1)} %get-tuple-element.610), channel_id=1, source_target_pairs={{32,0},{64,32},{96,64},{128,96},{160,128},{192,160},{224,192},{256... | collective-permute-start | bytes 1572872 | tf_op jit(solution)/shard_map/while/body/eval_jaxpr/ppermute | solution.py:12
  654.1 12.4 %collective-permute-done = bf16[64,4096]{1,0:T(8,128)(2,1)S(1)} collective-permute-done((bf16[64,4096]{1,0:T(8,128)(2,1)S(1)}, bf16[64,4096]{1,0:T(8,128)(2,1)S(1)}, u32[]{:S(2)}, u32[]{:S(2)}) %collective-permute-start) | collective-permute-done | bytes 524320 | tf_op jit(solution)/shard_map/while/body/eval_jaxpr/ppermute | solution.py:12
  666.6 2.6 fusion.38
  669.2 3.3 fusion.37
  672.5 350.7 %reduce-scatter.2.cloned.1.call-done = bf16[128,512]{1,0:T(8,128)(2,1)} async-done(((bf16[4096,512]{1,0:T(8,128)(2,1)}), bf16[128,512]{1,0:T(8,128)(2,1)}) %reduce-scatter.2.cloned.1.call-update) | async-done | bytes 131088 | tf_op jit(solution)/shard_map/reduce_scatter | solution.py:96
  1023.1 1.6 bitcast_convert_fusion
  (57 shorter events, 1.2 us)
Async XLA Ops:
  6.5 254.2 %copy-start.2 = (bf16[1,2,64,4096]{3,2,1,0:T(8,128)(2,1)S(1)}, bf16[1,2,64,4096]{3,2,1,0:T(8,128)(2,1)}, u32[]{:S(2)}) copy-start(bf16[1,2,64,4096]{3,2,1,0:T(8,128)(2,1)} %param.10) | copy-start | bytes 3145732
  6.5 251.9 %all-gather.3.cloned.1.call-start = ((), (), s32[]{:S(2)}) async-start(), calls=%async_computation.2 | async-start | bytes 4325376 | tf_op jit(solution)/shard_map/all_gather | solution.py:51
  7.3 1015.9 %reduce-scatter.2.cloned.1.call-start = ((), (), s32[]{:S(2)}) async-start(), calls=%async_computation.1 | async-start | bytes 4325376 | tf_op jit(solution)/shard_map/reduce_scatter | solution.py:96
  260.8 12.3 %collective-permute-start = (bf16[64,4096]{1,0:T(8,128)(2,1)S(1)}, bf16[64,4096]{1,0:T(8,128)(2,1)S(1)}, u32[]{:S(2)}, u32[]{:S(2)}) collective-permute-start(bf16[64,4096]{1,0:T(8,128)(2,1)S(1)} %get-tuple-element.610), channel_id=1, source_target_pairs={{32,0},{64,32},{96,64},{128,96},{160,128},{192,160},{224,192},{256... | collective-permute-start | bytes 1572872 | tf_op jit(solution)/shard_map/while/body/eval_jaxpr/ppermute | solution.py:12
  273.1 22.8 %collective-permute-start = (bf16[64,4096]{1,0:T(8,128)(2,1)S(1)}, bf16[64,4096]{1,0:T(8,128)(2,1)S(1)}, u32[]{:S(2)}, u32[]{:S(2)}) collective-permute-start(bf16[64,4096]{1,0:T(8,128)(2,1)S(1)} %get-tuple-element.610), channel_id=1, source_target_pairs={{32,0},{64,32},{96,64},{128,96},{160,128},{192,160},{224,192},{256... | collective-permute-start | bytes 1572872 | tf_op jit(solution)/shard_map/while/body/eval_jaxpr/ppermute | solution.py:12
  295.9 26.3 %collective-permute-start = (bf16[64,4096]{1,0:T(8,128)(2,1)S(1)}, bf16[64,4096]{1,0:T(8,128)(2,1)S(1)}, u32[]{:S(2)}, u32[]{:S(2)}) collective-permute-start(bf16[64,4096]{1,0:T(8,128)(2,1)S(1)} %get-tuple-element.610), channel_id=1, source_target_pairs={{32,0},{64,32},{96,64},{128,96},{160,128},{192,160},{224,192},{256... | collective-permute-start | bytes 1572872 | tf_op jit(solution)/shard_map/while/body/eval_jaxpr/ppermute | solution.py:12
  322.3 3.5 copy-start.3
  322.3 3.5 copy-start.5
  322.3 4.1 copy-start
  326.1 2.6 copy-start.4
  326.1 2.6 copy-start.6
  329.1 19.4 %collective-permute-start = (bf16[64,4096]{1,0:T(8,128)(2,1)S(1)}, bf16[64,4096]{1,0:T(8,128)(2,1)S(1)}, u32[]{:S(2)}, u32[]{:S(2)}) collective-permute-start(bf16[64,4096]{1,0:T(8,128)(2,1)S(1)} %get-tuple-element.610), channel_id=1, source_target_pairs={{32,0},{64,32},{96,64},{128,96},{160,128},{192,160},{224,192},{256... | collective-permute-start | bytes 1572872 | tf_op jit(solution)/shard_map/while/body/eval_jaxpr/ppermute | solution.py:12
  348.5 3.5 copy-start.3
  348.5 3.5 copy-start.5
  348.5 4.1 copy-start
  352.2 2.6 copy-start.4
  352.3 2.6 copy-start.6
  355.3 21.8 %collective-permute-start = (bf16[64,4096]{1,0:T(8,128)(2,1)S(1)}, bf16[64,4096]{1,0:T(8,128)(2,1)S(1)}, u32[]{:S(2)}, u32[]{:S(2)}) collective-permute-start(bf16[64,4096]{1,0:T(8,128)(2,1)S(1)} %get-tuple-element.610), channel_id=1, source_target_pairs={{32,0},{64,32},{96,64},{128,96},{160,128},{192,160},{224,192},{256... | collective-permute-start | bytes 1572872 | tf_op jit(solution)/shard_map/while/body/eval_jaxpr/ppermute | solution.py:12
  377.1 27.1 %collective-permute-start = (bf16[64,4096]{1,0:T(8,128)(2,1)S(1)}, bf16[64,4096]{1,0:T(8,128)(2,1)S(1)}, u32[]{:S(2)}, u32[]{:S(2)}) collective-permute-start(bf16[64,4096]{1,0:T(8,128)(2,1)S(1)} %get-tuple-element.610), channel_id=1, source_target_pairs={{32,0},{64,32},{96,64},{128,96},{160,128},{192,160},{224,192},{256... | collective-permute-start | bytes 1572872 | tf_op jit(solution)/shard_map/while/body/eval_jaxpr/ppermute | solution.py:12
  404.2 27.0 %collective-permute-start = (bf16[64,4096]{1,0:T(8,128)(2,1)S(1)}, bf16[64,4096]{1,0:T(8,128)(2,1)S(1)}, u32[]{:S(2)}, u32[]{:S(2)}) collective-permute-start(bf16[64,4096]{1,0:T(8,128)(2,1)S(1)} %get-tuple-element.610), channel_id=1, source_target_pairs={{32,0},{64,32},{96,64},{128,96},{160,128},{192,160},{224,192},{256... | collective-permute-start | bytes 1572872 | tf_op jit(solution)/shard_map/while/body/eval_jaxpr/ppermute | solution.py:12
  431.3 27.3 %collective-permute-start = (bf16[64,4096]{1,0:T(8,128)(2,1)S(1)}, bf16[64,4096]{1,0:T(8,128)(2,1)S(1)}, u32[]{:S(2)}, u32[]{:S(2)}) collective-permute-start(bf16[64,4096]{1,0:T(8,128)(2,1)S(1)} %get-tuple-element.610), channel_id=1, source_target_pairs={{32,0},{64,32},{96,64},{128,96},{160,128},{192,160},{224,192},{256... | collective-permute-start | bytes 1572872 | tf_op jit(solution)/shard_map/while/body/eval_jaxpr/ppermute | solution.py:12
  458.7 27.2 %collective-permute-start = (bf16[64,4096]{1,0:T(8,128)(2,1)S(1)}, bf16[64,4096]{1,0:T(8,128)(2,1)S(1)}, u32[]{:S(2)}, u32[]{:S(2)}) collective-permute-start(bf16[64,4096]{1,0:T(8,128)(2,1)S(1)} %get-tuple-element.610), channel_id=1, source_target_pairs={{32,0},{64,32},{96,64},{128,96},{160,128},{192,160},{224,192},{256... | collective-permute-start | bytes 1572872 | tf_op jit(solution)/shard_map/while/body/eval_jaxpr/ppermute | solution.py:12
  486.0 27.2 %collective-permute-start = (bf16[64,4096]{1,0:T(8,128)(2,1)S(1)}, bf16[64,4096]{1,0:T(8,128)(2,1)S(1)}, u32[]{:S(2)}, u32[]{:S(2)}) collective-permute-start(bf16[64,4096]{1,0:T(8,128)(2,1)S(1)} %get-tuple-element.610), channel_id=1, source_target_pairs={{32,0},{64,32},{96,64},{128,96},{160,128},{192,160},{224,192},{256... | collective-permute-start | bytes 1572872 | tf_op jit(solution)/shard_map/while/body/eval_jaxpr/ppermute | solution.py:12
  513.3 26.4 %collective-permute-start = (bf16[64,4096]{1,0:T(8,128)(2,1)S(1)}, bf16[64,4096]{1,0:T(8,128)(2,1)S(1)}, u32[]{:S(2)}, u32[]{:S(2)}) collective-permute-start(bf16[64,4096]{1,0:T(8,128)(2,1)S(1)} %get-tuple-element.610), channel_id=1, source_target_pairs={{32,0},{64,32},{96,64},{128,96},{160,128},{192,160},{224,192},{256... | collective-permute-start | bytes 1572872 | tf_op jit(solution)/shard_map/while/body/eval_jaxpr/ppermute | solution.py:12
  539.8 20.3 %collective-permute-start = (bf16[64,4096]{1,0:T(8,128)(2,1)S(1)}, bf16[64,4096]{1,0:T(8,128)(2,1)S(1)}, u32[]{:S(2)}, u32[]{:S(2)}) collective-permute-start(bf16[64,4096]{1,0:T(8,128)(2,1)S(1)} %get-tuple-element.610), channel_id=1, source_target_pairs={{32,0},{64,32},{96,64},{128,96},{160,128},{192,160},{224,192},{256... | collective-permute-start | bytes 1572872 | tf_op jit(solution)/shard_map/while/body/eval_jaxpr/ppermute | solution.py:12
  560.2 25.8 %collective-permute-start = (bf16[64,4096]{1,0:T(8,128)(2,1)S(1)}, bf16[64,4096]{1,0:T(8,128)(2,1)S(1)}, u32[]{:S(2)}, u32[]{:S(2)}) collective-permute-start(bf16[64,4096]{1,0:T(8,128)(2,1)S(1)} %get-tuple-element.610), channel_id=1, source_target_pairs={{32,0},{64,32},{96,64},{128,96},{160,128},{192,160},{224,192},{256... | collective-permute-start | bytes 1572872 | tf_op jit(solution)/shard_map/while/body/eval_jaxpr/ppermute | solution.py:12
  586.0 26.0 %collective-permute-start = (bf16[64,4096]{1,0:T(8,128)(2,1)S(1)}, bf16[64,4096]{1,0:T(8,128)(2,1)S(1)}, u32[]{:S(2)}, u32[]{:S(2)}) collective-permute-start(bf16[64,4096]{1,0:T(8,128)(2,1)S(1)} %get-tuple-element.610), channel_id=1, source_target_pairs={{32,0},{64,32},{96,64},{128,96},{160,128},{192,160},{224,192},{256... | collective-permute-start | bytes 1572872 | tf_op jit(solution)/shard_map/while/body/eval_jaxpr/ppermute | solution.py:12
  612.1 28.4 %collective-permute-start = (bf16[64,4096]{1,0:T(8,128)(2,1)S(1)}, bf16[64,4096]{1,0:T(8,128)(2,1)S(1)}, u32[]{:S(2)}, u32[]{:S(2)}) collective-permute-start(bf16[64,4096]{1,0:T(8,128)(2,1)S(1)} %get-tuple-element.610), channel_id=1, source_target_pairs={{32,0},{64,32},{96,64},{128,96},{160,128},{192,160},{224,192},{256... | collective-permute-start | bytes 1572872 | tf_op jit(solution)/shard_map/while/body/eval_jaxpr/ppermute | solution.py:12
  640.5 26.0 %collective-permute-start = (bf16[64,4096]{1,0:T(8,128)(2,1)S(1)}, bf16[64,4096]{1,0:T(8,128)(2,1)S(1)}, u32[]{:S(2)}, u32[]{:S(2)}) collective-permute-start(bf16[64,4096]{1,0:T(8,128)(2,1)S(1)} %get-tuple-element.610), channel_id=1, source_target_pairs={{32,0},{64,32},{96,64},{128,96},{160,128},{192,160},{224,192},{256... | collective-permute-start | bytes 1572872 | tf_op jit(solution)/shard_map/while/body/eval_jaxpr/ppermute | solution.py:12
  666.6 2.6 copy-start.7
Sparse Core Ops, SparseCore 0:
  9.4 248.9 all-gather.2
  672.6 350.4 reduce-scatter.1
where the time goes:
time: 1030 us
  waiting for transfers between devices  656 us (64%)
  starting transfers between devices  205 us (20%)
  blocking collectives  129 us (13%)
  matrix products  17 us (2%)
  between operations  14 us (1%)
    reduce_scatter x1, waiting for transfers between devices, shards(): lax.psum_scatter(partial_sum.astype(jnp.bfloat16), 'dp', scatter_dimensio...  351 us
    ppermute x16, starting transfers between devices, shifted(): return lax.ppermute(block, axis, route)  205 us
    ppermute x16, waiting for transfers between devices, shifted(): return lax.ppermute(block, axis, route)  186 us
    psum x1, blocking collectives, shards(): weight_total = lax.psum(jnp.sum(code_values), 'dp') / 127.0  129 us
    all_gather x1, waiting for transfers between devices, shards(): weight = lax.all_gather(proj_weight[0], 'dp', axis=0, tiled=True)  119 us
  transfers between devices with their start and end apart: 18, of which 18 were waited for; matrix products, arithmetic and copies ran while one was open for 0% of the time, Pallas kernels for 0%

commit v1 on v0

v1 whole, which is shorter than its diff:
```python
import jax
import jax.numpy as jnp
from jax import lax
from jax.experimental import pallas as pl
from jax.experimental.pallas import tpu as pltpu
from jax.sharding import PartitionSpec as P

MESH = pl.DeviceIdType.MESH
F32 = jnp.float32
BF16 = jnp.bfloat16
EPSILON = 1e-06
TOK = 64
WIDTH = 4096
HIDDEN = 512
ROWS = 128
CHUNKS = 8
COLS = WIDTH // CHUNKS
GROUPS = COLS // ROWS


def device(x, z, core, y):
    return (x * 4 + (z // 8) * 2 + core, y * 8 + z % 8)


def kernel(
    inputs, loss, codes, shard, out,
    weights, units, normed, grads, outgoing, factors, project, slope, inv_rms, partial,
    hop1, hop2p, hop2m, ringp, ringm, final, tally, tally_in, staged,
    local_sem, gather_recv, gather_z_send, gather_y_send, cross_send, cross_recv,
    chain_send, chain_recv, hop1_recv, hop2p_recv, hop2m_recv, ringp_recv, ringm_recv,
    sum_y_send, sum_z_send, final_send, final_recv, tally_send, tally_recv,
):
    section = lax.axis_index("section")
    group = lax.axis_index("dp")
    x, half, core = section // 4, (section // 2) % 2, section % 2
    y, low = group // 8, group % 8
    z = half * 8 + low
    sister = device(x, z, 1 - core, y)
    zdev = {s: device(x, (z + 16 + s) % 16, core, y) for s in (1, -1, 2, -2, 4, -4)}
    ydev = {s: device(x, z, core, (y + 4 + s) % 4) for s in (1, -1, 2)}
    home = core == half
    first = jnp.logical_and(x == 3, core == 1)
    last = jnp.logical_and(x == 0, core == 0)
    far = (z + 8) % 16
    next_x = device((x + 3) % 4, z, 1, y)
    prev_x = device((x + 1) % 4, z, 0, y)

    barrier = pltpu.get_barrier_semaphore()

    def greet(target):
        pl.semaphore_signal(barrier, inc=1, device_id=target, device_id_type=MESH)

    for s in (1, -1, 2, 4):
        greet(zdev[s])
    for s in (1, -1, 2):
        greet(ydev[s])
    greet(sister)

    @pl.when(jnp.logical_not(home))
    def _():
        greet(device(x, far, 0, y))
        greet(device(x, far, 1, y))

    @pl.when(jnp.logical_and(core == 1, x < 3))
    def _():
        greet(prev_x)

    pl.semaphore_wait(barrier, 9 + (1 - core) * ((x + 3) // 4))

    def remote(src, dst, send, recv, target):
        return pltpu.make_async_remote_copy(
            src_ref=src, dst_ref=dst, send_sem=send, recv_sem=recv,
            device_id=target, device_id_type=MESH,
        )

    here = y * 8 + low

    def own_weight():
        return pltpu.make_async_copy(shard.at[0], weights.at[core, here], local_sem.at[0])

    def lend_weight():
        return remote(
            shard.at[0], weights.at[core, here], cross_send.at[0],
            gather_recv.at[core, here], sister,
        )

    def own_inputs():
        return pltpu.make_async_copy(inputs.at[0, half], units.at[core], local_sem.at[1])

    def lend_inputs():
        return remote(
            inputs.at[0, half], units.at[core], cross_send.at[1], cross_recv.at[core], sister
        )

    def cross_inputs():
        return remote(
            inputs.at[0, 1 - half], units.at[core], cross_send.at[2], cross_recv.at[core],
            device(x, far, half, y),
        )

    def seed_copy():
        return pltpu.make_async_copy(loss.at[half], staged, local_sem.at[2])

    @pl.when(home)
    def _():
        own_weight().start()
        own_inputs().start()

    @pl.when(jnp.logical_not(home))
    def _():
        lend_weight().start()
        lend_inputs().start()

    cross_inputs().start()
    seed_copy().start()

    def block_ref(k, yy, ll):
        return weights.at[k, yy * 8 + ll]

    def gather_z(k, ll, sgn):
        return remote(
            block_ref(k, y, ll), block_ref(k, y, ll), gather_z_send.at[(1 - sgn) // 2, k, ll],
            gather_recv.at[k, y * 8 + ll], zdev[sgn],
        )

    def gather_y(k, yy, ll, sgn, slot):
        return remote(
            block_ref(k, yy, ll), block_ref(k, yy, ll), gather_y_send.at[slot, k, ll],
            gather_recv.at[k, yy * 8 + ll], ydev[sgn],
        )

    def arrived(k, yy, ll):
        remote(
            block_ref(k, yy, ll), block_ref(k, yy, ll), cross_send.at[0],
            gather_recv.at[k, yy * 8 + ll], sister,
        ).wait_recv()

    def side(ll):
        return 1 - 2 * (ll % 2)

    def ring_place(t, sgn):
        zz = (z + 16 - sgn * t) % 16
        return zz // 8 == core, zz % 8

    def spread_y(k, ll):
        gather_y(k, y, ll, 1, 0).start()
        gather_y(k, y, ll, -1, 1).start()

    @pl.when(home)
    def _():
        own_weight().wait()

        def begin(k):
            for sgn in (1, -1):
                gather_z(k, low, sgn).start()
            spread_y(k, low)

        begin(core)
        arrived(1 - core, y, low)
        begin(1 - core)

    def relay_y(t, sgn):
        valid, ll = ring_place(t, sgn)
        valid = jnp.logical_and(valid, jnp.logical_or(t < 8, side(ll) == sgn))

        @pl.when(valid)
        def _():
            for k in (1, 0):
                arrived(k, (y + 3) % 4, ll)

                @pl.when(side(ll) == 1)
                def _():
                    gather_y(k, (y + 3) % 4, ll, 1, 2).start()

                arrived(k, (y + 1) % 4, ll)

                @pl.when(side(ll) == -1)
                def _():
                    gather_y(k, (y + 1) % 4, ll, -1, 2).start()

    def relay_z(t, sgn):
        valid, ll = ring_place(t, sgn)
        valid = jnp.logical_and(valid, jnp.logical_or(t < 8, side(ll) == sgn))
        onward = jnp.logical_or(t < 7, jnp.logical_and(t == 7, side(ll) == sgn))

        @pl.when(valid)
        def _():
            for k in (1, 0):
                arrived(k, y, ll)

                @pl.when(onward)
                def _():
                    gather_z(k, ll, sgn).start()

                spread_y(k, ll)

    def gather_step(t, carry):
        for sgn in (1, -1):
            relay_z(t, sgn)

        @pl.when(t == 1)
        def _():
            relay_y(0, 1)

        @pl.when(t > 1)
        def _():
            for sgn in (1, -1):
                relay_y(t - 1, sgn)

        return carry

    lax.fori_loop(1, 9, gather_step, 0)
    for sgn in (1, -1):
        relay_y(8, sgn)

    tally[0] = jnp.broadcast_to(
        jnp.sum(codes[0] + codes[1], axis=0, keepdims=True), (8, 128)
    )
    for i, target in enumerate((zdev[-1], zdev[-2], zdev[-4], ydev[-1], ydev[2])):
        copy = remote(tally.at[i], tally_in.at[i], tally_send.at[i], tally_recv.at[i], target)
        copy.start()
        copy.wait()
        tally[i + 1] = tally[i] + tally_in[i]

    seed_copy().wait()

    @pl.when(first)
    def _():
        scale = codes[half, :, 0:1] / 127.0
        for j in range(CHUNKS):
            part = staged[:, j * COLS:(j + 1) * COLS].astype(F32)
            grads[1, j] = (part * scale).astype(BF16)

    @pl.when(home)
    def _():
        own_inputs().wait()

    def inputs_arrived(k):
        remote(
            units.at[k], units.at[k], cross_send.at[1], cross_recv.at[k], sister
        ).wait_recv()

    @pl.when(home)
    def _():
        inputs_arrived(1 - core)

    @pl.when(jnp.logical_not(home))
    def _():
        inputs_arrived(0)
        inputs_arrived(1)

    def far_arrived(ll, carry):
        for k in (1, 0):
            arrived(k, (y + 2) % 4, ll)
        return carry

    lax.fori_loop(0, 8, far_arrived, 0)

    def weight_chunk(k, j):
        return weights[k, pl.ds(j * GROUPS, GROUPS)].reshape(COLS, HIDDEN)

    def columns(ref, k, j):
        return ref[k, :, pl.ds(pl.multiple_of(j * COLS, COLS), COLS)]

    def prepare(k):
        def square(j, acc):
            v = columns(units, k, j).astype(F32)
            return acc + jnp.sum(v * v, axis=-1, keepdims=True)

        total = lax.fori_loop(0, CHUNKS, square, jnp.zeros((TOK, 1), F32))
        inv = lax.rsqrt(total / WIDTH + EPSILON)
        inv_rms[k] = jnp.broadcast_to(inv, (TOK, 128))

        def multiply(j, acc):
            row = (columns(units, k, j).astype(F32) * inv).astype(BF16)
            normed[k, :, pl.ds(pl.multiple_of(j * COLS, COLS), COLS)] = row
            return acc + jnp.dot(row, weight_chunk(k, j), preferred_element_type=F32)

        value = lax.fori_loop(0, CHUNKS, multiply, jnp.zeros((TOK, HIDDEN), F32))
        prob = jax.nn.sigmoid(value)
        project[k] = value
        slope[k] = prob * (1.0 + value * (1.0 - prob))
        factors[k, TOK:] = (value * prob).astype(BF16)

    for k in (1, 0):
        prepare(k)

    def chain(j, target):
        return remote(outgoing.at[j], grads.at[1, j], chain_send.at[j], chain_recv.at[j], target)

    def stage(k):
        def act_grad(j, acc):
            if k == 1:
                @pl.when(jnp.logical_not(first))
                def _():
                    chain(j, sister).wait_recv()
            return acc + jnp.dot(grads[k, j], weight_chunk(k, j), preferred_element_type=F32)

        grad_act = lax.fori_loop(0, CHUNKS, act_grad, jnp.zeros((TOK, HIDDEN), F32))
        grad_proj = (grad_act * slope[k]).astype(BF16)
        factors[k, :TOK] = grad_proj
        mean = jnp.sum(grad_proj.astype(F32) * project[k], axis=-1, keepdims=True) / WIDTH
        inv = inv_rms[k, :, 0:1]

        def in_grad(j, carry):
            norm = lax.dot_general(
                grad_proj, weight_chunk(k, j), (((1,), (1,)), ((), ())),
                preferred_element_type=F32,
            )
            unit = columns(units, k, j).astype(F32) * inv
            result = (grads[k, j].astype(F32) + inv * (norm - unit * mean)).astype(BF16)
            if k == 1:
                grads[0, j] = result
            else:
                outgoing[j] = result

                @pl.when(core == 1)
                def _():
                    chain(j, sister).start()

                @pl.when(core == 0)
                def _():
                    chain(j, next_x).start()

            return carry

        def onward():
            lax.fori_loop(0, CHUNKS, in_grad, 0)

        if k == 1:
            onward()
        else:
            pl.when(jnp.logical_not(last))(onward)

    stage(1)
    stage(0)

    def weight_grad(k):
        def rows(j, carry):
            left = jnp.concatenate([columns(normed, k, j), grads[k, j]], axis=0)
            term = lax.dot_general(
                left, factors[k], (((0,), (0,)), ((), ())), preferred_element_type=F32
            )
            partial[k, pl.ds(j * GROUPS, GROUPS)] = term.astype(BF16).reshape(
                GROUPS, ROWS, HIDDEN
            )
            return carry

        lax.fori_loop(0, CHUNKS, rows, 0)

    def part_ref(k, dy, ll):
        return partial.at[k, ((y + 4 + dy) % 4) * 8 + ll]

    def send_hop1(k, ll, sgn):
        return remote(
            part_ref(k, 2, ll), hop1.at[k, ll], sum_y_send.at[0, k, ll], hop1_recv.at[k, ll],
            ydev[sgn],
        )

    def send_hop2(k, ll, sgn):
        land, sem = (hop2p, hop2p_recv) if sgn == 1 else (hop2m, hop2m_recv)
        return remote(
            part_ref(k, sgn, ll), land.at[k, ll], sum_y_send.at[(3 - sgn) // 2, k, ll],
            sem.at[k, ll], ydev[sgn],
        )

    def send_ring(k, ll, sgn):
        land, sem = (ringp, ringp_recv) if sgn == 1 else (ringm, ringm_recv)
        return remote(
            part_ref(k, 0, ll), land.at[k, ll], sum_z_send.at[k, ll], sem.at[k, ll], zdev[sgn]
        )

    def target_place(t, sgn):
        zz = (z + 16 + sgn * t) % 16
        ll = zz % 8
        valid = jnp.logical_and(zz // 8 == core, jnp.logical_or(t < 8, side(ll) == sgn))
        return valid, ll

    def begin_y(k, t, sgn):
        valid, ll = target_place(t, sgn)

        @pl.when(valid)
        def _():
            @pl.when(side(ll) == 1)
            def _():
                send_hop1(k, ll, 1).start()
                send_hop2(k, ll, -1).start()

            @pl.when(side(ll) == -1)
            def _():
                send_hop1(k, ll, -1).start()
                send_hop2(k, ll, 1).start()

    def begin_sum(k):
        def body(i, carry):
            for sgn in (1, -1):
                begin_y(k, 8 - i, sgn)
            return carry

        lax.fori_loop(0, 8, body, 0)
        begin_y(k, 0, 1)

    def add_into(k, dy, ll, extra):
        index = ((y + 4 + dy) % 4) * 8 + ll
        value = partial[k, index].astype(F32)
        for ref in extra:
            value = value + ref[k, ll].astype(F32)
        partial[k, index] = value.astype(BF16)

    def middle_y(t, sgn):
        valid, ll = target_place(t, sgn)

        @pl.when(valid)
        def _():
            for k in (1, 0):
                send_hop1(k, ll, 1).wait_recv()

                @pl.when(side(ll) == 1)
                def _():
                    add_into(k, 1, ll, (hop1,))
                    send_hop2(k, ll, 1).start()

                @pl.when(side(ll) == -1)
                def _():
                    add_into(k, -1, ll, (hop1,))
                    send_hop2(k, ll, -1).start()

    def ring_sum(t, sgn):
        valid, ll = target_place(t, sgn)
        fed = jnp.logical_or(t < 7, jnp.logical_and(t == 7, side(ll) == sgn))
        land = ringp if sgn == 1 else ringm

        @pl.when(valid)
        def _():
            for k in (1, 0):
                send_hop2(k, ll, 1).wait_recv()
                send_hop2(k, ll, -1).wait_recv()

                @pl.when(fed)
                def _():
                    send_ring(k, ll, sgn).wait_recv()
                    add_into(k, 0, ll, (hop2p, hop2m, land))

                @pl.when(jnp.logical_not(fed))
                def _():
                    add_into(k, 0, ll, (hop2p, hop2m))

                send_ring(k, ll, sgn).start()

    for k in (1, 0):
        weight_grad(k)
        begin_sum(k)

    def sum_step(i, carry):
        @pl.when(i < 8)
        def _():
            for sgn in (1, -1):
                middle_y(8 - i, sgn)

        @pl.when(i == 8)
        def _():
            middle_y(0, 1)

        @pl.when(jnp.logical_and(i >= 1, i < 9))
        def _():
            for sgn in (1, -1):
                ring_sum(9 - i, sgn)

        return carry

    lax.fori_loop(0, 9, sum_step, 0)

    scale = 127.0 / tally[5, 0:1, 0:1]

    def send_final():
        return remote(final.at[0], final.at[1], final_send.at[0], final_recv.at[0], sister)

    @pl.when(home)
    def _():
        def total(k):
            for sgn in (1, -1):
                send_hop2(k, low, sgn).wait_recv()
                send_ring(k, low, sgn).wait_recv()
            value = partial[k, here].astype(F32)
            for ref in (hop2p, hop2m, ringp, ringm):
                value = value + ref[k, low].astype(F32)
            return value

        final[0] = total(1 - core)
        send_final().start()
        out[0] = total(core) * scale
        send_final().wait_send()

    @pl.when(jnp.logical_not(home))
    def _():
        send_final().wait_recv()
        out[0] = final[1] * scale

    @pl.when(jnp.logical_not(home))
    def _():
        lend_weight().wait_send()
        lend_inputs().wait_send()

    cross_inputs().wait_send()

    @pl.when(jnp.logical_not(last))
    def _():
        for j in range(CHUNKS):
            chain(j, sister).wait_send()

    def settle(ll, carry):
        zz = core * 8 + ll
        ahead = (z + 16 - zz) % 16
        plus = jnp.logical_or(ahead < 7, jnp.logical_and(ahead == 7, side(ll) == 1))
        back = (16 - ahead) % 16
        minus = jnp.logical_or(back < 7, jnp.logical_and(back == 7, side(ll) == -1))
        for k in (1, 0):
            @pl.when(plus)
            def _():
                gather_z(k, ll, 1).wait_send()

            @pl.when(minus)
            def _():
                gather_z(k, ll, -1).wait_send()

            gather_y(k, y, ll, 1, 0).wait_send()
            gather_y(k, y, ll, -1, 1).wait_send()
            gather_y(k, y, ll, 1, 2).wait_send()
            send_hop1(k, ll, 1).wait_send()
            send_hop2(k, ll, 1).wait_send()
            send_hop2(k, ll, -1).wait_send()

            @pl.when(ahead != 0)
            def _():
                send_ring(k, ll, 1).wait_send()

        return carry

    lax.fori_loop(0, 8, settle, 0)


def shards(section_inputs, loss_grads, weight_codes, proj_weight):
    codes = jnp.broadcast_to(weight_codes.astype(F32)[:, :, None], (2, TOK, 128))
    anywhere = pl.BlockSpec(memory_space=pl.ANY)
    vmem = pl.BlockSpec(memory_space=pltpu.VMEM)
    dma = pltpu.SemaphoreType.DMA
    blocks = (2, 8, ROWS, HIDDEN)
    return pl.pallas_call(
        kernel,
        out_shape=jax.ShapeDtypeStruct((1, ROWS, HIDDEN), F32),
        in_specs=[anywhere, anywhere, vmem, vmem],
        out_specs=vmem,
        scratch_shapes=[
            pltpu.VMEM((2, 32, ROWS, HIDDEN), BF16),
            pltpu.VMEM((2, TOK, WIDTH), BF16),
            pltpu.VMEM((2, TOK, WIDTH), BF16),
            pltpu.VMEM((2, CHUNKS, TOK, COLS), BF16),
            pltpu.VMEM((CHUNKS, TOK, COLS), BF16),
            pltpu.VMEM((2, 2 * TOK, HIDDEN), BF16),
            pltpu.VMEM((2, TOK, HIDDEN), F32),
            pltpu.VMEM((2, TOK, HIDDEN), F32),
            pltpu.VMEM((2, TOK, 128), F32),
            pltpu.VMEM((2, 32, ROWS, HIDDEN), BF16),
            pltpu.VMEM(blocks, BF16),
            pltpu.VMEM(blocks, BF16),
            pltpu.VMEM(blocks, BF16),
            pltpu.VMEM(blocks, BF16),
            pltpu.VMEM(blocks, BF16),
            pltpu.VMEM((2, ROWS, HIDDEN), F32),
            pltpu.VMEM((6, 8, 128), F32),
            pltpu.VMEM((5, 8, 128), F32),
            pltpu.VMEM((TOK, WIDTH), BF16),
            dma((3,)),
            dma((2, 32)),
            dma((2, 2, 8)),
            dma((3, 2, 8)),
            dma((3,)),
            dma((2,)),
            dma((CHUNKS,)),
            dma((CHUNKS,)),
            dma((2, 8)),
            dma((2, 8)),
            dma((2, 8)),
            dma((2, 8)),
            dma((2, 8)),
            dma((3, 2, 8)),
            dma((2, 8)),
            dma((1,)),
            dma((1,)),
            dma((5,)),
            dma((5,)),
        ],
        compiler_params=pltpu.CompilerParams(
            collective_id=0, has_side_effects=True, vmem_limit_bytes=56 * 2**20
        ),
    )(section_inputs[0][None], loss_grads, codes, proj_weight)


def solution(mesh):
    return jax.shard_map(
        shards,
        mesh=mesh,
        in_specs=(
            P("section", None, "dp", None),
            P(None, "dp", None),
            P(None, "dp"),
            P("section", "dp", None),
        ),
        out_specs=P("section", "dp", None),
        check_vma=False,
    )
```

time: 1030 us -> 321 us (0.31)
  the two profiles are of different devices: /device:TPU:6 before, /device:TPU:1 now
where the time goes in v1:
time: 321 us
  Pallas kernels  318 us (99%)
    pallas_call x1, Pallas kernels, shards(): pl.pallas_call(kernel, out_shape=jax.ShapeDtypeStruct((1, ROWS, HIDDEN),...  318 us

profile of v1, /device:TPU:1, one launch (start us, length us, event | category | flops | bytes accessed | tf_op | source)
XLA Modules:
  0.0 320.6 jit_solution(9687853272665585405)
XLA Ops:
  0.0 0.7 convert_element_type.3
  0.7 0.7 broadcast_in_dim.2.codes
  1.4 317.6 %shard_map.46 = f32[1,128,512]{2,1,0:T(8,128)} custom-call(bf16[1,2,64,4096]{3,2,1,0:T(8,128)(2,1)} %inputs.1, bf16[2,64,4096]{2,1,0:T(8,128)(2,1)} %loss.1, f32[2,64,128]{2,1,0:T(8,128)} %broadcast_in_dim.2.codes, bf16[1,128,512]{2,1,0:T(8,128)(2,1)} %shard.1), custom_call_target="tpu_custom_call" | custom-call | tf_op jit(solution)/shard_map/pallas_call | solution.py:548
  319.0 1.7 copy.6

commit v2 on v1

--- a/solution.py
+++ b/solution.py
@@ -25,7 +25,7 @@
 def kernel(
     inputs, loss, codes, shard, out,
     weights, units, normed, grads, outgoing, factors, project, slope, inv_rms, partial,
-    hop1, hop2p, hop2m, ringp, ringm, final, tally, tally_in, staged,
+    hop1, hop2p, hop2m, ringp, ringm, final, tally, staged,
     local_sem, gather_recv, gather_z_send, gather_y_send, cross_send, cross_recv,
     chain_send, chain_recv, hop1_recv, hop2p_recv, hop2m_recv, ringp_recv, ringm_recv,
     sum_y_send, sum_z_send, final_send, final_recv, tally_send, tally_recv,
@@ -36,8 +36,8 @@
     y, low = group // 8, group % 8
     z = half * 8 + low
     sister = device(x, z, 1 - core, y)
-    zdev = {s: device(x, (z + 16 + s) % 16, core, y) for s in (1, -1, 2, -2, 4, -4)}
-    ydev = {s: device(x, z, core, (y + 4 + s) % 4) for s in (1, -1, 2)}
+    zdev = {s: device(x, (z + 16 + s) % 16, core, y) for s in (1, -1)}
+    ydev = {s: device(x, z, core, (y + 4 + s) % 4) for s in (1, -1)}
     home = core == half
     first = jnp.logical_and(x == 3, core == 1)
     last = jnp.logical_and(x == 0, core == 0)
@@ -50,9 +50,8 @@
     def greet(target):
         pl.semaphore_signal(barrier, inc=1, device_id=target, device_id_type=MESH)
 
-    for s in (1, -1, 2, 4):
+    for s in (1, -1):
         greet(zdev[s])
-    for s in (1, -1, 2):
         greet(ydev[s])
     greet(sister)
 
@@ -65,7 +64,7 @@
     def _():
         greet(prev_x)
 
-    pl.semaphore_wait(barrier, 9 + (1 - core) * ((x + 3) // 4))
+    pl.semaphore_wait(barrier, 6 + (1 - core) * ((x + 3) // 4))
 
     def remote(src, dst, send, recv, target):
         return pltpu.make_async_remote_copy(
@@ -92,10 +91,11 @@
             inputs.at[0, half], units.at[core], cross_send.at[1], cross_recv.at[core], sister
         )
 
-    def cross_inputs():
-        return remote(
-            inputs.at[0, 1 - half], units.at[core], cross_send.at[2], cross_recv.at[core],
-            device(x, far, half, y),
+    def cross_inputs(first_row, rows):
+        part = pl.ds(first_row, rows)
+        return remote(
+            inputs.at[0, 1 - half, part], units.at[core, part], cross_send.at[2],
+            cross_recv.at[core], device(x, far, half, y),
         )
 
     def seed_copy():
@@ -111,7 +111,6 @@
         lend_weight().start()
         lend_inputs().start()
 
-    cross_inputs().start()
     seed_copy().start()
 
     def block_ref(k, yy, ll):
@@ -194,7 +193,26 @@
 
                 spread_y(k, ll)
 
+    def pass_tally(slot, target):
+        return remote(
+            tally.at[slot], tally.at[slot + 1], tally_send.at[slot], tally_recv.at[slot + 1],
+            target,
+        )
+
+    tally[0] = jnp.broadcast_to(
+        jnp.sum(codes[0] + codes[1], axis=0, keepdims=True), (8, 128)
+    )
+    pass_tally(0, zdev[1]).start()
+
+    def tally_y(slot):
+        pass_tally(slot - 1, ydev[1]).wait_recv()
+        pass_tally(slot, ydev[1]).start()
+
     def gather_step(t, carry):
+        @pl.when(t % 2 == 1)
+        def _():
+            cross_inputs(((t - 1) // 2) * (TOK // 4), TOK // 4).start()
+
         for sgn in (1, -1):
             relay_z(t, sgn)
 
@@ -206,6 +224,11 @@
         def _():
             for sgn in (1, -1):
                 relay_y(t - 1, sgn)
+
+        @pl.when(t < 7)
+        def _():
+            pass_tally(t - 1, zdev[1]).wait_recv()
+            pass_tally(t, zdev[1]).start()
 
         return carry
 
@@ -213,14 +236,9 @@
     for sgn in (1, -1):
         relay_y(8, sgn)
 
-    tally[0] = jnp.broadcast_to(
-        jnp.sum(codes[0] + codes[1], axis=0, keepdims=True), (8, 128)
-    )
-    for i, target in enumerate((zdev[-1], zdev[-2], zdev[-4], ydev[-1], ydev[2])):
-        copy = remote(tally.at[i], tally_in.at[i], tally_send.at[i], tally_recv.at[i], target)
-        copy.start()
-        copy.wait()
-        tally[i + 1] = tally[i] + tally_in[i]
+    pass_tally(6, zdev[1]).wait_recv()
+    tally[8] = sum(tally[i] for i in range(1, 8)) + tally[0]
+    pass_tally(8, ydev[1]).start()
 
     seed_copy().wait()
 
@@ -257,26 +275,31 @@
     lax.fori_loop(0, 8, far_arrived, 0)
 
     def weight_chunk(k, j):
-        return weights[k, pl.ds(j * GROUPS, GROUPS)].reshape(COLS, HIDDEN)
+        return weights[k, j * GROUPS:(j + 1) * GROUPS].reshape(COLS, HIDDEN)
 
     def columns(ref, k, j):
-        return ref[k, :, pl.ds(pl.multiple_of(j * COLS, COLS), COLS)]
+        return ref[k, :, j * COLS:(j + 1) * COLS]
+
+    def unrolled(body, carry):
+        for j in range(CHUNKS):
+            carry = body(j, carry)
+        return carry
 
     def prepare(k):
         def square(j, acc):
             v = columns(units, k, j).astype(F32)
             return acc + jnp.sum(v * v, axis=-1, keepdims=True)
 
-        total = lax.fori_loop(0, CHUNKS, square, jnp.zeros((TOK, 1), F32))
+        total = unrolled(square, jnp.zeros((TOK, 1), F32))
         inv = lax.rsqrt(total / WIDTH + EPSILON)
         inv_rms[k] = jnp.broadcast_to(inv, (TOK, 128))
 
         def multiply(j, acc):
             row = (columns(units, k, j).astype(F32) * inv).astype(BF16)
-            normed[k, :, pl.ds(pl.multiple_of(j * COLS, COLS), COLS)] = row
+            normed[k, :, j * COLS:(j + 1) * COLS] = row
             return acc + jnp.dot(row, weight_chunk(k, j), preferred_element_type=F32)
 
-        value = lax.fori_loop(0, CHUNKS, multiply, jnp.zeros((TOK, HIDDEN), F32))
+        value = unrolled(multiply, jnp.zeros((TOK, HIDDEN), F32))
         prob = jax.nn.sigmoid(value)
         project[k] = value
         slope[k] = prob * (1.0 + value * (1.0 - prob))
@@ -296,7 +319,7 @@
                     chain(j, sister).wait_recv()
             return acc + jnp.dot(grads[k, j], weight_chunk(k, j), preferred_element_type=F32)
 
-        grad_act = lax.fori_loop(0, CHUNKS, act_grad, jnp.zeros((TOK, HIDDEN), F32))
+        grad_act = unrolled(act_grad, jnp.zeros((TOK, HIDDEN), F32))
         grad_proj = (grad_act * slope[k]).astype(BF16)
         factors[k, :TOK] = grad_proj
         mean = jnp.sum(grad_proj.astype(F32) * project[k], axis=-1, keepdims=True) / WIDTH
@@ -325,7 +348,7 @@
             return carry
 
         def onward():
-            lax.fori_loop(0, CHUNKS, in_grad, 0)
+            unrolled(in_grad, 0)
 
         if k == 1:
             onward()
@@ -333,7 +356,9 @@
             pl.when(jnp.logical_not(last))(onward)
 
     stage(1)
+    tally_y(9)
     stage(0)
+    tally_y(10)
 
     def weight_grad(k):
         def rows(j, carry):
@@ -341,12 +366,12 @@
             term = lax.dot_general(
                 left, factors[k], (((0,), (0,)), ((), ())), preferred_element_type=F32
             )
-            partial[k, pl.ds(j * GROUPS, GROUPS)] = term.astype(BF16).reshape(
+            partial[k, j * GROUPS:(j + 1) * GROUPS] = term.astype(BF16).reshape(
                 GROUPS, ROWS, HIDDEN
             )
             return carry
 
-        lax.fori_loop(0, CHUNKS, rows, 0)
+        unrolled(rows, 0)
 
     def part_ref(k, dy, ll):
         return partial.at[k, ((y + 4 + dy) % 4) * 8 + ll]
@@ -470,7 +495,8 @@
 
     lax.fori_loop(0, 9, sum_step, 0)
 
-    scale = 127.0 / tally[5, 0:1, 0:1]
+    pass_tally(10, ydev[1]).wait_recv()
+    scale = 127.0 / sum(tally[i] for i in range(8, 12))[0:1, 0:1]
 
     def send_final():
         return remote(final.at[0], final.at[1], final_send.at[0], final_recv.at[0], sister)
@@ -501,12 +527,15 @@
         lend_weight().wait_send()
         lend_inputs().wait_send()
 
-    cross_inputs().wait_send()
+    cross_inputs(0, TOK).wait_send()
 
     @pl.when(jnp.logical_not(last))
     def _():
         for j in range(CHUNKS):
             chain(j, sister).wait_send()
+
+    for i in (0, 1, 2, 3, 4, 5, 6, 8, 9, 10):
+        pass_tally(i, sister).wait_send()
 
     def settle(ll, carry):
         zz = core * 8 + ll
@@ -567,8 +596,7 @@
             pltpu.VMEM(blocks, BF16),
             pltpu.VMEM(blocks, BF16),
             pltpu.VMEM((2, ROWS, HIDDEN), F32),
-            pltpu.VMEM((6, 8, 128), F32),
-            pltpu.VMEM((5, 8, 128), F32),
+            pltpu.VMEM((12, 8, 128), F32),
             pltpu.VMEM((TOK, WIDTH), BF16),
             dma((3,)),
             dma((2, 32)),
@@ -587,8 +615,8 @@
             dma((2, 8)),
             dma((1,)),
             dma((1,)),
-            dma((5,)),
-            dma((5,)),
+            dma((12,)),
+            dma((12,)),
         ],
         compiler_params=pltpu.CompilerParams(
             collective_id=0, has_side_effects=True, vmem_limit_bytes=56 * 2**20

time: 321 us -> 273 us (0.85)
  Pallas kernels: 318 us -> 269 us
    pallas_call x1, Pallas kernels: 318 us -> 269 us  [shards(): pl.pallas_call(kernel, out_shape=jax.ShapeDtypeStruct((1, ROWS, HIDDEN),...]
where the time goes in v2:
time: 273 us; the launch traced here: 272 us
  Pallas kernels  269 us (99%)
    pallas_call x1, Pallas kernels, shards(): pl.pallas_call(kernel, out_shape=jax.ShapeDtypeStruct((1, ROWS, HIDDEN),...  269 us

profile of v2, /device:TPU:1, one launch (start us, length us, event | category | flops | bytes accessed | tf_op | source)
XLA Modules:
  0.0 272.4 jit_solution(7525578452470886140)
XLA Ops:
  0.0 0.7 convert_element_type.3
  0.7 0.7 broadcast_in_dim.2.codes
  1.4 269.3 %shard_map.46 = f32[1,128,512]{2,1,0:T(8,128)} custom-call(bf16[1,2,64,4096]{3,2,1,0:T(8,128)(2,1)} %inputs.1, bf16[2,64,4096]{2,1,0:T(8,128)(2,1)} %loss.1, f32[2,64,128]{2,1,0:T(8,128)} %broadcast_in_dim.2.codes, bf16[1,128,512]{2,1,0:T(8,128)(2,1)} %shard.1), custom_call_target="tpu_custom_call" | custom-call | tf_op jit(solution)/shard_map/pallas_call | solution.py:577
  270.8 1.7 copy.6

commit v3 on v2

--- a/solution.py
+++ b/solution.py
@@ -16,6 +16,9 @@
 CHUNKS = 8
 COLS = WIDTH // CHUNKS
 GROUPS = COLS // ROWS
+SPLIT = 384
+REST = HIDDEN - SPLIT
+AHEAD = 1
 
 
 def device(x, z, core, y):
@@ -24,10 +27,11 @@
 
 def kernel(
     inputs, loss, codes, shard, out,
-    weights, units, normed, grads, outgoing, factors, project, slope, inv_rms, partial,
-    hop1, hop2p, hop2m, ringp, ringm, final, tally, staged,
+    weights, units, normed, grads, outgoing, factors, project, slope, inv_rms, partial, wide,
+    hop1, hop2p, hop2m, ringp, ringm, widep, widem, end1, end2p, end2m, final, tally, staged,
     local_sem, gather_recv, gather_z_send, gather_y_send, cross_send, cross_recv,
     chain_send, chain_recv, hop1_recv, hop2p_recv, hop2m_recv, ringp_recv, ringm_recv,
+    widep_recv, widem_recv, end1_recv, end2p_recv, end2m_recv, wide_send, end_send,
     sum_y_send, sum_z_send, final_send, final_recv, tally_send, tally_recv,
 ):
     section = lax.axis_index("section")
@@ -366,9 +370,12 @@
             term = lax.dot_general(
                 left, factors[k], (((0,), (0,)), ((), ())), preferred_element_type=F32
             )
-            partial[k, j * GROUPS:(j + 1) * GROUPS] = term.astype(BF16).reshape(
-                GROUPS, ROWS, HIDDEN
-            )
+            term = term.astype(BF16)
+            for i in range(GROUPS):
+                place = j * GROUPS + i
+                block = term[i * ROWS:(i + 1) * ROWS]
+                partial[k, place] = block[:, :SPLIT]
+                wide[k, place % 8, place // 8] = block[:, SPLIT:]
             return carry
 
         unrolled(rows, 0)
@@ -422,8 +429,7 @@
                 begin_y(k, 8 - i, sgn)
             return carry
 
-        lax.fori_loop(0, 8, body, 0)
-        begin_y(k, 0, 1)
+        lax.fori_loop(0, AHEAD, body, 0)
 
     def add_into(k, dy, ll, extra):
         index = ((y + 4 + dy) % 4) * 8 + ll
@@ -472,13 +478,80 @@
 
                 send_ring(k, ll, sgn).start()
 
+    def send_wide(k, ll, sgn):
+        land, sem = (widep, widep_recv) if sgn == 1 else (widem, widem_recv)
+        return remote(
+            wide.at[k, ll], land.at[k, ll], wide_send.at[k, ll], sem.at[k, ll], zdev[sgn]
+        )
+
+    def ring_wide(t, sgn):
+        valid, ll = target_place(t, sgn)
+        fed = jnp.logical_or(t < 7, jnp.logical_and(t == 7, side(ll) == sgn))
+        land = widep if sgn == 1 else widem
+
+        @pl.when(valid)
+        def _():
+            for k in (1, 0):
+                @pl.when(fed)
+                def _():
+                    send_wide(k, ll, sgn).wait_recv()
+                    wide[k, ll] = (wide[k, ll].astype(F32) + land[k, ll].astype(F32)).astype(BF16)
+
+                send_wide(k, ll, sgn).start()
+
+    def end_ref(k, dy):
+        return wide.at[k, low, (y + 4 + dy) % 4]
+
+    def send_end1(k):
+        sgn = 2 * k - 1
+        return remote(end_ref(k, 2), end1.at[k], end_send.at[0, k], end1_recv.at[k], ydev[sgn])
+
+    def send_end2(k, sgn):
+        land, sem = (end2p, end2p_recv) if sgn == 1 else (end2m, end2m_recv)
+        return remote(
+            end_ref(k, sgn), land.at[k], end_send.at[(3 - sgn) // 2, k], sem.at[k], ydev[sgn]
+        )
+
+    def end_wide():
+        for k in (1, 0):
+            send_wide(k, low, 1).wait_recv()
+            send_wide(k, low, -1).wait_recv()
+            value = wide[k, low].astype(F32)
+            for ref in (widep, widem):
+                value = value + ref[k, low].astype(F32)
+            wide[k, low] = value.astype(BF16)
+            send_end1(k).start()
+            send_end2(k, 1 - 2 * k).start()
+        for k in (1, 0):
+            sgn = 2 * k - 1
+            send_end1(k).wait_recv()
+            place = (y + 4 + sgn) % 4
+            value = wide[k, low, place].astype(F32) + end1[k].astype(F32)
+            wide[k, low, place] = value.astype(BF16)
+            send_end2(k, sgn).start()
+
     for k in (1, 0):
         weight_grad(k)
         begin_sum(k)
 
     def sum_step(i, carry):
+        later = 8 - AHEAD - i
+
+        @pl.when(later >= 1)
+        def _():
+            for k in (1, 0):
+                for sgn in (1, -1):
+                    begin_y(k, later, sgn)
+
+        @pl.when(later == 0)
+        def _():
+            for k in (1, 0):
+                begin_y(k, 0, 1)
+
         @pl.when(i < 8)
         def _():
+            for sgn in (1, -1):
+                ring_wide(8 - i, sgn)
             for sgn in (1, -1):
                 middle_y(8 - i, sgn)
 
@@ -494,6 +567,7 @@
         return carry
 
     lax.fori_loop(0, 9, sum_step, 0)
+    pl.when(home)(end_wide)
 
     pass_tally(10, ydev[1]).wait_recv()
     scale = 127.0 / sum(tally[i] for i in range(8, 12))[0:1, 0:1]
@@ -503,24 +577,30 @@
 
     @pl.when(home)
     def _():
-        def total(k):
+        def total(k, put):
             for sgn in (1, -1):
                 send_hop2(k, low, sgn).wait_recv()
                 send_ring(k, low, sgn).wait_recv()
             value = partial[k, here].astype(F32)
             for ref in (hop2p, hop2m, ringp, ringm):
                 value = value + ref[k, low].astype(F32)
-            return value
-
-        final[0] = total(1 - core)
+            send_end2(k, 1).wait_recv()
+            send_end2(k, -1).wait_recv()
+            rest = wide[k, low, y].astype(F32)
+            for ref in (end2p, end2m):
+                rest = rest + ref[k].astype(F32)
+            put[0, :, :SPLIT] = value * scale
+            put[0, :, SPLIT:] = rest * scale
+
+        total(1 - core, final)
         send_final().start()
-        out[0] = total(core) * scale
+        total(core, out)
         send_final().wait_send()
 
     @pl.when(jnp.logical_not(home))
     def _():
         send_final().wait_recv()
-        out[0] = final[1] * scale
+        out[0] = final[1]
 
     @pl.when(jnp.logical_not(home))
     def _():
@@ -536,6 +616,13 @@
 
     for i in (0, 1, 2, 3, 4, 5, 6, 8, 9, 10):
         pass_tally(i, sister).wait_send()
+
+    @pl.when(home)
+    def _():
+        for k in (1, 0):
+            send_end1(k).wait_send()
+            send_end2(k, 1).wait_send()
+            send_end2(k, -1).wait_send()
 
     def settle(ll, carry):
         zz = core * 8 + ll
@@ -562,6 +649,7 @@
             @pl.when(ahead != 0)
             def _():
                 send_ring(k, ll, 1).wait_send()
+                send_wide(k, ll, 1).wait_send()
 
         return carry
 
@@ -573,7 +661,9 @@
     anywhere = pl.BlockSpec(memory_space=pl.ANY)
     vmem = pl.BlockSpec(memory_space=pltpu.VMEM)
     dma = pltpu.SemaphoreType.DMA
-    blocks = (2, 8, ROWS, HIDDEN)
+    blocks = (2, 8, ROWS, SPLIT)
+    slabs = (2, 8, 4, ROWS, REST)
+    ends = (2, ROWS, REST)
     return pl.pallas_call(
         kernel,
         out_shape=jax.ShapeDtypeStruct((1, ROWS, HIDDEN), F32),
@@ -589,12 +679,18 @@
             pltpu.VMEM((2, TOK, HIDDEN), F32),
             pltpu.VMEM((2, TOK, HIDDEN), F32),
             pltpu.VMEM((2, TOK, 128), F32),
-            pltpu.VMEM((2, 32, ROWS, HIDDEN), BF16),
+            pltpu.VMEM((2, 32, ROWS, SPLIT), BF16),
+            pltpu.VMEM(slabs, BF16),
             pltpu.VMEM(blocks, BF16),
             pltpu.VMEM(blocks, BF16),
             pltpu.VMEM(blocks, BF16),
             pltpu.VMEM(blocks, BF16),
             pltpu.VMEM(blocks, BF16),
+            pltpu.VMEM(slabs, BF16),
+            pltpu.VMEM(slabs, BF16),
+            pltpu.VMEM(ends, BF16),
+            pltpu.VMEM(ends, BF16),
+            pltpu.VMEM(ends, BF16),
             pltpu.VMEM((2, ROWS, HIDDEN), F32),
             pltpu.VMEM((12, 8, 128), F32),
             pltpu.VMEM((TOK, WIDTH), BF16),
@@ -611,6 +707,13 @@
             dma((2, 8)),
             dma((2, 8)),
             dma((2, 8)),
+            dma((2, 8)),
+            dma((2, 8)),
+            dma((2,)),
+            dma((2,)),
+            dma((2,)),
+            dma((2, 8)),
+            dma((3, 2)),
             dma((3, 2, 8)),
             dma((2, 8)),
             dma((1,)),

time: 273 us -> 244 us (0.89)
  Pallas kernels: 269 us -> 241 us
    pallas_call x1, Pallas kernels: 269 us -> 241 us  [shards(): pl.pallas_call(kernel, out_shape=jax.ShapeDtypeStruct((1, ROWS, HIDDEN),...]
where the time goes in v3:
time: 244 us
  Pallas kernels  241 us (99%)
    pallas_call x1, Pallas kernels, shards(): pl.pallas_call(kernel, out_shape=jax.ShapeDtypeStruct((1, ROWS, HIDDEN),...  241 us

profile of v3, /device:TPU:1, one launch (start us, length us, event | category | flops | bytes accessed | tf_op | source)
XLA Modules:
  0.0 243.6 jit_solution(3078213022864054446)
XLA Ops:
  0.0 0.7 convert_element_type.3
  0.7 0.7 broadcast_in_dim.2.codes
  1.4 240.5 %shard_map.46 = f32[1,128,512]{2,1,0:T(8,128)} custom-call(bf16[1,2,64,4096]{3,2,1,0:T(8,128)(2,1)} %inputs.1, bf16[2,64,4096]{2,1,0:T(8,128)(2,1)} %loss.1, f32[2,64,128]{2,1,0:T(8,128)} %broadcast_in_dim.2.codes, bf16[1,128,512]{2,1,0:T(8,128)(2,1)} %shard.1), custom_call_target="tpu_custom_call" | custom-call | tf_op jit(solution)/shard_map/pallas_call | solution.py:667
  241.9 1.7 copy.6

commit v4 on v3

--- a/solution.py
+++ b/solution.py
@@ -10,6 +10,8 @@
 BF16 = jnp.bfloat16
 EPSILON = 1e-06
 TOK = 64
+WAVES = 2
+PART = TOK // WAVES
 WIDTH = 4096
 HIDDEN = 512
 ROWS = 128
@@ -27,7 +29,7 @@
 
 def kernel(
     inputs, loss, codes, shard, out,
-    weights, units, normed, grads, outgoing, factors, project, slope, inv_rms, partial, wide,
+    weights, units, normed, grads, outgoing, factors, project, slope, inv_rms, flipped, partial, wide,
     hop1, hop2p, hop2m, ringp, ringm, widep, widem, end1, end2p, end2m, final, tally, staged,
     local_sem, gather_recv, gather_z_send, gather_y_send, cross_send, cross_recv,
     chain_send, chain_recv, hop1_recv, hop2p_recv, hop2m_recv, ringp_recv, ringm_recv,
@@ -68,6 +70,42 @@
     def _():
         greet(prev_x)
 
+    here = y * 8 + low
+
+    def own_weight():
+        return pltpu.make_async_copy(shard.at[0], weights.at[core, here], local_sem.at[0])
+
+    def own_inputs():
+        return pltpu.make_async_copy(inputs.at[0, half], units.at[core], local_sem.at[1])
+
+    def seed_copy():
+        return pltpu.make_async_copy(loss.at[half], staged, local_sem.at[2])
+
+    @pl.when(home)
+    def _():
+        own_weight().start()
+        own_inputs().start()
+
+    seed_copy().start()
+    values = codes[...].astype(F32)
+    tally[0] = jnp.broadcast_to(
+        jnp.sum(jnp.sum(values, axis=1, keepdims=True), axis=0, keepdims=True), (8, 128)
+    )
+    seed_copy().wait()
+
+    @pl.when(first)
+    def _():
+        row = jnp.where(half == 0, values[0:1], values[1:2])
+        grid = (TOK, TOK)
+        diagonal = lax.broadcasted_iota(jnp.int32, grid, 0) == lax.broadcasted_iota(
+            jnp.int32, grid, 1
+        )
+        spread_row = jnp.broadcast_to(row, grid)
+        scale = jnp.sum(jnp.where(diagonal, spread_row, 0.0), axis=1, keepdims=True) / 127.0
+        for j in range(CHUNKS):
+            part = staged[:, j * COLS:(j + 1) * COLS].astype(F32)
+            grads[1, j] = (part * scale).astype(BF16)
+
     pl.semaphore_wait(barrier, 6 + (1 - core) * ((x + 3) // 4))
 
     def remote(src, dst, send, recv, target):
@@ -76,20 +114,12 @@
             device_id=target, device_id_type=MESH,
         )
 
-    here = y * 8 + low
-
-    def own_weight():
-        return pltpu.make_async_copy(shard.at[0], weights.at[core, here], local_sem.at[0])
-
     def lend_weight():
         return remote(
             shard.at[0], weights.at[core, here], cross_send.at[0],
             gather_recv.at[core, here], sister,
         )
 
-    def own_inputs():
-        return pltpu.make_async_copy(inputs.at[0, half], units.at[core], local_sem.at[1])
-
     def lend_inputs():
         return remote(
             inputs.at[0, half], units.at[core], cross_send.at[1], cross_recv.at[core], sister
@@ -102,20 +132,10 @@
             cross_recv.at[core], device(x, far, half, y),
         )
 
-    def seed_copy():
-        return pltpu.make_async_copy(loss.at[half], staged, local_sem.at[2])
-
-    @pl.when(home)
-    def _():
-        own_weight().start()
-        own_inputs().start()
-
     @pl.when(jnp.logical_not(home))
     def _():
         lend_weight().start()
         lend_inputs().start()
-
-    seed_copy().start()
 
     def block_ref(k, yy, ll):
         return weights.at[k, yy * 8 + ll]
@@ -203,9 +223,6 @@
             target,
         )
 
-    tally[0] = jnp.broadcast_to(
-        jnp.sum(codes[0] + codes[1], axis=0, keepdims=True), (8, 128)
-    )
     pass_tally(0, zdev[1]).start()
 
     def tally_y(slot):
@@ -213,7 +230,7 @@
         pass_tally(slot, ydev[1]).start()
 
     def gather_step(t, carry):
-        @pl.when(t % 2 == 1)
+        @pl.when(jnp.logical_and(core == 1, t % 2 == 1))
         def _():
             cross_inputs(((t - 1) // 2) * (TOK // 4), TOK // 4).start()
 
@@ -237,6 +254,11 @@
         return carry
 
     lax.fori_loop(1, 9, gather_step, 0)
+
+    @pl.when(core == 0)
+    def _():
+        cross_inputs(0, TOK).start()
+
     for sgn in (1, -1):
         relay_y(8, sgn)
 
@@ -244,32 +266,18 @@
     tally[8] = sum(tally[i] for i in range(1, 8)) + tally[0]
     pass_tally(8, ydev[1]).start()
 
-    seed_copy().wait()
-
-    @pl.when(first)
-    def _():
-        scale = codes[half, :, 0:1] / 127.0
-        for j in range(CHUNKS):
-            part = staged[:, j * COLS:(j + 1) * COLS].astype(F32)
-            grads[1, j] = (part * scale).astype(BF16)
-
-    @pl.when(home)
-    def _():
-        own_inputs().wait()
-
-    def inputs_arrived(k):
-        remote(
-            units.at[k], units.at[k], cross_send.at[1], cross_recv.at[k], sister
-        ).wait_recv()
-
-    @pl.when(home)
-    def _():
-        inputs_arrived(1 - core)
-
-    @pl.when(jnp.logical_not(home))
-    def _():
-        inputs_arrived(0)
-        inputs_arrived(1)
+    def ready(k):
+        local = jnp.logical_and(home, core == k)
+
+        @pl.when(local)
+        def _():
+            own_inputs().wait()
+
+        @pl.when(jnp.logical_not(local))
+        def _():
+            remote(
+                units.at[k], units.at[k], cross_send.at[1], cross_recv.at[k], sister
+            ).wait_recv()
 
     def far_arrived(ll, carry):
         for k in (1, 0):
@@ -289,7 +297,13 @@
             carry = body(j, carry)
         return carry
 
+    def flip(k):
+        for j in range(CHUNKS):
+            flipped[k, j] = weight_chunk(k, j).T
+
     def prepare(k):
+        ready(k)
+
         def square(j, acc):
             v = columns(units, k, j).astype(F32)
             return acc + jnp.sum(v * v, axis=-1, keepdims=True)
@@ -309,59 +323,88 @@
         slope[k] = prob * (1.0 + value * (1.0 - prob))
         factors[k, TOK:] = (value * prob).astype(BF16)
 
-    for k in (1, 0):
-        prepare(k)
-
-    def chain(j, target):
-        return remote(outgoing.at[j], grads.at[1, j], chain_send.at[j], chain_recv.at[j], target)
-
-    def stage(k):
+    prepare(1)
+
+    @pl.when(jnp.logical_not(first))
+    def _():
+        prepare(0)
+        flip(1)
+        flip(0)
+
+    def rows_of(w):
+        return slice(w * PART, (w + 1) * PART)
+
+    def chain(w, j, target):
+        part = pl.ds(w * PART, PART)
+        return remote(
+            outgoing.at[j, part], grads.at[1, j, part], chain_send.at[w, j],
+            chain_recv.at[w, j], target,
+        )
+
+    def stage(k, w):
+        part = rows_of(w)
+
         def act_grad(j, acc):
             if k == 1:
                 @pl.when(jnp.logical_not(first))
                 def _():
-                    chain(j, sister).wait_recv()
-            return acc + jnp.dot(grads[k, j], weight_chunk(k, j), preferred_element_type=F32)
-
-        grad_act = unrolled(act_grad, jnp.zeros((TOK, HIDDEN), F32))
-        grad_proj = (grad_act * slope[k]).astype(BF16)
-        factors[k, :TOK] = grad_proj
-        mean = jnp.sum(grad_proj.astype(F32) * project[k], axis=-1, keepdims=True) / WIDTH
-        inv = inv_rms[k, :, 0:1]
-
-        def in_grad(j, carry):
-            norm = lax.dot_general(
+                    chain(w, j, sister).wait_recv()
+            return acc + jnp.dot(
+                grads[k, j, part], weight_chunk(k, j), preferred_element_type=F32
+            )
+
+        grad_act = unrolled(act_grad, jnp.zeros((PART, HIDDEN), F32))
+        grad_proj = (grad_act * slope[k, part]).astype(BF16)
+        factors[k, part] = grad_proj
+        mean = jnp.sum(grad_proj.astype(F32) * project[k, part], axis=-1, keepdims=True) / WIDTH
+        inv = inv_rms[k, part, 0:1]
+
+        def straight(j):
+            return lax.dot_general(
                 grad_proj, weight_chunk(k, j), (((1,), (1,)), ((), ())),
                 preferred_element_type=F32,
             )
-            unit = columns(units, k, j).astype(F32) * inv
-            result = (grads[k, j].astype(F32) + inv * (norm - unit * mean)).astype(BF16)
+
+        def turned(j):
+            return jnp.dot(grad_proj, flipped[k, j], preferred_element_type=F32)
+
+        def in_grad(j, product):
+            norm = product(j)
+            unit = units[k, part, j * COLS:(j + 1) * COLS].astype(F32) * inv
+            result = (grads[k, j, part].astype(F32) + inv * (norm - unit * mean)).astype(BF16)
             if k == 1:
-                grads[0, j] = result
+                grads[0, j, part] = result
             else:
-                outgoing[j] = result
+                outgoing[j, part] = result
 
                 @pl.when(core == 1)
                 def _():
-                    chain(j, sister).start()
+                    chain(w, j, sister).start()
 
                 @pl.when(core == 0)
                 def _():
-                    chain(j, next_x).start()
-
-            return carry
-
-        def onward():
-            unrolled(in_grad, 0)
-
-        if k == 1:
-            onward()
-        else:
-            pl.when(jnp.logical_not(last))(onward)
-
-    stage(1)
+                    chain(w, j, next_x).start()
+
+            return product
+
+        @pl.when(first)
+        def _():
+            unrolled(in_grad, straight)
+
+        @pl.when(jnp.logical_and(jnp.logical_not(first), jnp.logical_or(k == 1, jnp.logical_not(last))))
+        def _():
+            unrolled(in_grad, turned)
+
+    stage(1, 0)
+
+    @pl.when(first)
+    def _():
+        prepare(0)
+
+    stage(0, 0)
     tally_y(9)
-    stage(0)
+    stage(1, 1)
+    stage(0, 1)
     tally_y(10)
 
     def weight_grad(k):
@@ -611,8 +654,9 @@
 
     @pl.when(jnp.logical_not(last))
     def _():
-        for j in range(CHUNKS):
-            chain(j, sister).wait_send()
+        for w in range(WAVES):
+            for j in range(CHUNKS):
+                chain(w, j, sister).wait_send()
 
     for i in (0, 1, 2, 3, 4, 5, 6, 8, 9, 10):
         pass_tally(i, sister).wait_send()
@@ -657,7 +701,6 @@
 
 
 def shards(section_inputs, loss_grads, weight_codes, proj_weight):
-    codes = jnp.broadcast_to(weight_codes.astype(F32)[:, :, None], (2, TOK, 128))
     anywhere = pl.BlockSpec(memory_space=pl.ANY)
     vmem = pl.BlockSpec(memory_space=pltpu.VMEM)
     dma = pltpu.SemaphoreType.DMA
@@ -679,6 +722,7 @@
             pltpu.VMEM((2, TOK, HIDDEN), F32),
             pltpu.VMEM((2, TOK, HIDDEN), F32),
             pltpu.VMEM((2, TOK, 128), F32),
+            pltpu.VMEM((2, CHUNKS, HIDDEN, COLS), BF16),
             pltpu.VMEM((2, 32, ROWS, SPLIT), BF16),
             pltpu.VMEM(slabs, BF16),
             pltpu.VMEM(blocks, BF16),
@@ -700,8 +744,8 @@
             dma((3, 2, 8)),
             dma((3,)),
             dma((2,)),
-            dma((CHUNKS,)),
-            dma((CHUNKS,)),
+            dma((WAVES, CHUNKS)),
+            dma((WAVES, CHUNKS)),
             dma((2, 8)),
             dma((2, 8)),
             dma((2, 8)),
@@ -724,7 +768,7 @@
         compiler_params=pltpu.CompilerParams(
             collective_id=0, has_side_effects=True, vmem_limit_bytes=56 * 2**20
         ),
-    )(section_inputs[0][None], loss_grads, codes, proj_weight)
+    )(section_inputs[0][None], loss_grads, weight_codes, proj_weight)
 
 
 def solution(mesh):

time: 244 us -> 235 us (0.963)
  Pallas kernels: 241 us -> 233 us
    pallas_call x1, Pallas kernels: 241 us -> 233 us  [shards(): pl.pallas_call(kernel, out_shape=jax.ShapeDtypeStruct((1, ROWS, HIDDEN),...]
where the time goes in v4:
time: 235 us
  Pallas kernels  233 us (99%)
    pallas_call x1, Pallas kernels, shards(): pl.pallas_call(kernel, out_shape=jax.ShapeDtypeStruct((1, ROWS, HIDDEN),...  233 us

profile of v4, /device:TPU:1, one launch (start us, length us, event | category | flops | bytes accessed | tf_op | source)
XLA Modules:
  0.0 234.7 jit_solution(14075587404765544911)
XLA Ops:
  0.0 233.1 %shard_map.46 = f32[1,128,512]{2,1,0:T(8,128)} custom-call(bf16[1,2,64,4096]{3,2,1,0:T(8,128)(2,1)} %inputs.1, bf16[2,64,4096]{2,1,0:T(8,128)(2,1)} %loss.1, s32[2,64]{1,0:T(2,128)} %codes.1, bf16[1,128,512]{2,1,0:T(8,128)(2,1)} %shard.1), custom_call_target="tpu_custom_call" | custom-call | tf_op jit(solution)/shard_map/pallas_call | solution.py:710
  233.1 1.7 copy.6

commit v5 on v4

--- a/solution.py
+++ b/solution.py
@@ -128,7 +128,7 @@
     def cross_inputs(first_row, rows):
         part = pl.ds(first_row, rows)
         return remote(
-            inputs.at[0, 1 - half, part], units.at[core, part], cross_send.at[2],
+            inputs.at[0, 1 - half, :, part], units.at[core, :, part], cross_send.at[2],
             cross_recv.at[core], device(x, far, half, y),
         )
 
@@ -230,9 +230,9 @@
         pass_tally(slot, ydev[1]).start()
 
     def gather_step(t, carry):
-        @pl.when(jnp.logical_and(core == 1, t % 2 == 1))
-        def _():
-            cross_inputs(((t - 1) // 2) * (TOK // 4), TOK // 4).start()
+        @pl.when(core == 1)
+        def _():
+            cross_inputs((t - 1) * COLS, COLS).start()
 
         for sgn in (1, -1):
             relay_z(t, sgn)
@@ -257,7 +257,7 @@
 
     @pl.when(core == 0)
     def _():
-        cross_inputs(0, TOK).start()
+        cross_inputs(0, WIDTH).start()
 
     for sgn in (1, -1):
         relay_y(8, sgn)
@@ -327,9 +327,9 @@
 
     @pl.when(jnp.logical_not(first))
     def _():
-        prepare(0)
         flip(1)
         flip(0)
+        prepare(0)
 
     def rows_of(w):
         return slice(w * PART, (w + 1) * PART)
@@ -565,6 +565,8 @@
             wide[k, low] = value.astype(BF16)
             send_end1(k).start()
             send_end2(k, 1 - 2 * k).start()
+
+    def end_wide_later():
         for k in (1, 0):
             sgn = 2 * k - 1
             send_end1(k).wait_recv()
@@ -578,19 +580,6 @@
         begin_sum(k)
 
     def sum_step(i, carry):
-        later = 8 - AHEAD - i
-
-        @pl.when(later >= 1)
-        def _():
-            for k in (1, 0):
-                for sgn in (1, -1):
-                    begin_y(k, later, sgn)
-
-        @pl.when(later == 0)
-        def _():
-            for k in (1, 0):
-                begin_y(k, 0, 1)
-
         @pl.when(i < 8)
         def _():
             for sgn in (1, -1):
@@ -598,6 +587,21 @@
             for sgn in (1, -1):
                 middle_y(8 - i, sgn)
 
+        later = 8 - AHEAD - i
+
+        @pl.when(later >= 1)
+        def _():
+            for k in (1, 0):
+                for sgn in (1, -1):
+                    begin_y(k, later, sgn)
+
+        @pl.when(later == 0)
+        def _():
+            for k in (1, 0):
+                begin_y(k, 0, 1)
+
+        pl.when(jnp.logical_and(i == 8, home))(end_wide)
+
         @pl.when(i == 8)
         def _():
             middle_y(0, 1)
@@ -610,7 +614,7 @@
         return carry
 
     lax.fori_loop(0, 9, sum_step, 0)
-    pl.when(home)(end_wide)
+    pl.when(home)(end_wide_later)
 
     pass_tally(10, ydev[1]).wait_recv()
     scale = 127.0 / sum(tally[i] for i in range(8, 12))[0:1, 0:1]
@@ -650,7 +654,7 @@
         lend_weight().wait_send()
         lend_inputs().wait_send()
 
-    cross_inputs(0, TOK).wait_send()
+    cross_inputs(0, WIDTH).wait_send()
 
     @pl.when(jnp.logical_not(last))
     def _():

time: 235 us -> 231 us (0.983)
  Pallas kernels: 233 us -> 229 us
    pallas_call x1, Pallas kernels: 233 us -> 229 us  [shards(): pl.pallas_call(kernel, out_shape=jax.ShapeDtypeStruct((1, ROWS, HIDDEN),...]
where the time goes in v5:
time: 231 us
  Pallas kernels  229 us (99%)
    pallas_call x1, Pallas kernels, shards(): pl.pallas_call(kernel, out_shape=jax.ShapeDtypeStruct((1, ROWS, HIDDEN),...  229 us

profile of v5, /device:TPU:1, one launch (start us, length us, event | category | flops | bytes accessed | tf_op | source)
XLA Modules:
  0.0 230.5 jit_solution(4235881108610901408)
XLA Ops:
  0.0 228.8 %shard_map.46 = f32[1,128,512]{2,1,0:T(8,128)} custom-call(bf16[1,2,64,4096]{3,2,1,0:T(8,128)(2,1)} %inputs.1, bf16[2,64,4096]{2,1,0:T(8,128)(2,1)} %loss.1, s32[2,64]{1,0:T(2,128)} %codes.1, bf16[1,128,512]{2,1,0:T(8,128)(2,1)} %shard.1), custom_call_target="tpu_custom_call" | custom-call | tf_op jit(solution)/shard_map/pallas_call | solution.py:714
  228.8 1.7 copy.6

commit v6 on v5

--- a/solution.py
+++ b/solution.py
@@ -587,6 +587,17 @@
             for sgn in (1, -1):
                 middle_y(8 - i, sgn)
 
+        pl.when(jnp.logical_and(i == 8, home))(end_wide)
+
+        @pl.when(i == 8)
+        def _():
+            middle_y(0, 1)
+
+        @pl.when(jnp.logical_and(i >= 1, i < 9))
+        def _():
+            for sgn in (1, -1):
+                ring_sum(9 - i, sgn)
+
         later = 8 - AHEAD - i
 
         @pl.when(later >= 1)
@@ -599,17 +610,6 @@
         def _():
             for k in (1, 0):
                 begin_y(k, 0, 1)
-
-        pl.when(jnp.logical_and(i == 8, home))(end_wide)
-
-        @pl.when(i == 8)
-        def _():
-            middle_y(0, 1)
-
-        @pl.when(jnp.logical_and(i >= 1, i < 9))
-        def _():
-            for sgn in (1, -1):
-                ring_sum(9 - i, sgn)
 
         return carry
 

time: 231 us -> 229 us (level)
  no operation moved by 1% of the time
where the time goes in v6:
time: 229 us
  Pallas kernels  227 us (99%)
    pallas_call x1, Pallas kernels, shards(): pl.pallas_call(kernel, out_shape=jax.ShapeDtypeStruct((1, ROWS, HIDDEN),...  227 us

profile of v6, /device:TPU:1, one launch (start us, length us, event | category | flops | bytes accessed | tf_op | source)
XLA Modules:
  0.0 228.9 jit_solution(4584468036957945710)
XLA Ops:
  0.0 227.3 %shard_map.46 = f32[1,128,512]{2,1,0:T(8,128)} custom-call(bf16[1,2,64,4096]{3,2,1,0:T(8,128)(2,1)} %inputs.1, bf16[2,64,4096]{2,1,0:T(8,128)(2,1)} %loss.1, s32[2,64]{1,0:T(2,128)} %codes.1, bf16[1,128,512]{2,1,0:T(8,128)(2,1)} %shard.1), custom_call_target="tpu_custom_call" | custom-call | tf_op jit(solution)/shard_map/pallas_call | solution.py:714
  227.3 1.7 copy.6
